TPU v7x, 512 devices: a whole 4x4x16 slice. The times are simulated.
512 devices in a mesh: dp: 32 (over z, core), tensor: 16 (over x, y).
Axes of the slice: x: 4, y: 4, z: 16, core: 2. Of those that a mesh axis runs over, the one named last changes fastest.
Arguments:
- queries: bfloat16 [128, 16, 16384], P('dp', None, 'tensor'), may hold values from -18 to 18
- tree_kv: bfloat16 [128, 16, 8, 256], P('dp'), may hold values from -20 to 20
- prefix_kv: bfloat16 [32, 16, 1024, 256], P('dp', 'tensor'), may hold values from -20 to 20
- request_holder: int32 [128], replicated, may hold values from 0 to 31, as said below
- parents: int32 [128, 16], replicated, may hold values from 0 to 14, as said below
- out_weight: bfloat16 [16384, 16384], P('tensor', 'dp'), may hold values from -0.5 to 0.5
Outputs:
- projected: bfloat16 [128, 16, 16384], P('tensor', None, 'dp')
Inputs may be any that keep to these rules, and one draw needn't show every extreme that they name: `request_holder`: each group serves at most 16 requests, and one group serves exactly 16. parents[r, 0] = 0 and parents[r, i] < i for i >= 1.
All inputs are finite; a program needn't handle non-finite values.
Results may differ from a plain program's by a relative error of at most 0.01785.
Values may be sent and summed in bfloat16 or wider, within the bound.
No kernel may reach another device: no remote copies, remote signals or barrier semaphores. Data moves between devices by JAX's collectives and lax.ppermute only.
A program may use at most 64 MiB of HBM per device.

v0:
```python
import math

import jax
import jax.numpy as jnp
from jax import lax
from jax.sharding import PartitionSpec as P

CAP = 16


def swapped(x, axis, bit):
    return lax.ppermute(x, axis, [(i, i ^ 1 << bit) for i in range(lax.axis_size(axis))])


def ancestors(parents):
    count = parents.shape[-1]
    ident = jnp.eye(count, dtype=jnp.int32)
    upward = (parents[..., None] == jnp.arange(count, dtype=jnp.int32)[None, None, :]).astype(
        jnp.int32
    )
    reach = jnp.minimum(ident[None] + upward, 1)
    for level in range(4):
        reach = jnp.minimum(jnp.einsum("rij,rjk->rik", reach, reach), 1)
    return reach


def prefix_state(grouped, block):
    width = block.shape[-1] // 2
    scale = 1.0 / math.sqrt(width)
    scores = (
        jnp.einsum("snhd,pd->snhp", grouped, block[:, :width], preferred_element_type=jnp.float32)
        * scale
    )
    top = jnp.max(scores, axis=-1)
    weights = jnp.exp(scores - top[..., None])
    total = jnp.sum(weights, axis=-1)
    summed = jnp.einsum(
        "snhp,pd->snhd",
        weights.astype(jnp.bfloat16),
        block[:, width:],
        preferred_element_type=jnp.float32,
    )
    return (top, total, summed)


def combine_states(first, second):
    top = jnp.maximum(first[0], second[0])
    left = jnp.exp(first[0] - top)
    right = jnp.exp(second[0] - top)
    total = first[1] * left + second[1] * right
    summed = first[2] * left[..., None] + second[2] * right[..., None]
    return (top, total, summed)


def local(queries, tree_kv, prefix_kv, request_holder, parents, out_weight):
    group = lax.axis_index("dp")
    lane = lax.axis_index("tensor")
    lanes = lax.axis_size("tensor")
    width = tree_kv.shape[-1] // 2
    nodes = queries.shape[1]
    heads_here = queries.shape[2] // width
    tree_local = lax.dynamic_index_in_dim(tree_kv, lane // 2, 2, keepdims=False)
    all_queries, all_tree = (
        lax.all_gather(queries, "dp", axis=0, tiled=True),
        lax.all_gather(tree_local, "dp", axis=0, tiled=True),
    )
    requests = request_holder.shape[0]
    capacity = CAP
    order = jnp.arange(requests, dtype=jnp.int32)
    same = request_holder[:, None] == request_holder[None, :]
    earlier = order[None, :] < order[:, None]
    rank = jnp.sum((same & earlier).astype(jnp.int32), axis=1)
    slots = jnp.arange(capacity, dtype=jnp.int32)
    pick = (request_holder[None, :] == group) & (rank[None, :] == slots[:, None])
    pick_b = pick.astype(jnp.bfloat16)
    slot_queries = jnp.einsum(
        "sr,rnk->snk", pick_b, all_queries, preferred_element_type=jnp.float32
    ).astype(jnp.bfloat16)
    slot_tree = jnp.einsum(
        "sr,rnk->snk", pick_b, all_tree, preferred_element_type=jnp.float32
    ).astype(jnp.bfloat16)
    reach = ancestors(parents)
    slot_reach = jnp.einsum("sr,rij->sij", pick.astype(jnp.int32), reach)
    grouped = slot_queries.reshape(capacity, nodes, heads_here, width)
    own_half = prefix_kv[0, 0]
    other_half = swapped(own_half, "tensor", 0)
    state = prefix_state(grouped, jnp.concatenate([own_half, other_half], axis=0))
    scale = 1.0 / math.sqrt(width)
    tree_scores = (
        jnp.einsum(
            "snhd,sjd->snhj", grouped, slot_tree[..., :width], preferred_element_type=jnp.float32
        )
        * scale
    )
    mask = (slot_reach > 0)[:, :, None, :]
    tree_scores = jnp.where(mask, tree_scores, jnp.float32(-1e30))
    tree_top = jnp.max(tree_scores, axis=-1)
    tree_w = jnp.exp(tree_scores - tree_top[..., None]) * mask.astype(jnp.float32)
    tree_sum = jnp.einsum(
        "snhj,sjd->snhd",
        tree_w.astype(jnp.bfloat16),
        slot_tree[..., width:],
        preferred_element_type=jnp.float32,
    )
    top, total, summed = combine_states(state, (tree_top, jnp.sum(tree_w, axis=-1), tree_sum))
    attended = (
        (summed / total[..., None])
        .reshape(capacity, nodes, heads_here * width)
        .astype(jnp.bfloat16)
    )
    every = lax.all_gather(attended, "dp", axis=0, tiled=True)
    rows = jnp.take(every, request_holder * capacity + rank, axis=0)
    flat = rows.reshape(requests * nodes, heads_here * width)
    share = lax.psum_scatter(
        jnp.dot(flat, out_weight, preferred_element_type=jnp.float32).astype(jnp.bfloat16),
        "tensor",
        scatter_dimension=0,
        tiled=True,
    ).astype(jnp.float32)
    return share.reshape(requests // lanes, nodes, out_weight.shape[1]).astype(jnp.bfloat16)


def solution(mesh):
    return jax.shard_map(
        local,
        mesh=mesh,
        in_specs=(
            P("dp", None, "tensor"),
            P("dp", None, None, None),
            P("dp", "tensor", None, None),
            P(),
            P(),
            P("tensor", "dp"),
        ),
        out_specs=P("tensor", None, "dp"),
        check_vma=False,
    )
```

profile of v0, /device:TPU:1, one launch (start us, length us, event | category | flops | bytes accessed | tf_op | source)
XLA Modules:
  0.0 391.0 jit_solution(14717649948718874862)
XLA Ops:
  6.5 0.0 copy-start
  6.5 0.0 all-gather.9.cloned.1.call-start
  6.5 1.1 constant_dynamic-slice_fusion
  7.7 0.6 copy.53
  8.3 0.0 all-gather.9.cloned.1.call-update
  8.3 0.0 all-gather.5.cloned.1.call-start
  8.3 0.7 all-gather.5.cloned.1.call-update
  9.1 0.0 all-gather.7.cloned.1.call-start
  9.1 4.0 %collective-permute-start = (bf16[1024,256]{1,0:T(8,128)(2,1)}, bf16[1024,256]{1,0:T(8,128)(2,1)}, u32[]{:S(2)}, u32[]{:S(2)}) collective-permute-start(bf16[1024,256]{1,0:T(8,128)(2,1)} %bitcast.45), channel_id=1, source_target_pairs={{0,1},{1,0},{2,3},{3,2},{4,5},{5,4},{6,7},{7,6},{8,9},{9,8},{10,11... | collective-permute-start | bytes 1572872 | tf_op jit(solution)/shard_map/ppermute | solution.py:12
  13.1 0.8 copy.36
  14.0 0.9 convert_reduce_fusion
  14.9 0.7 compare_and_fusion
  15.5 6.9 %convolution_minimum_fusion.2 = s32[128,16,16]{2,1,0:T(8,128)S(1)} fusion(s32[128,16]{1,0:T(8,128)S(1)} %copy.36, s32[16,16]{1,0:T(8,128)S(1)} %fusion.55), kind=kOutput, calls=%fused_computation.12 | convolution fusion | flops 2293760 | bytes 140288 | tf_op jit(solution)/shard_map/rij,rjk->rik/dot_general | solution.py:23
  22.4 6.3 %convolution_minimum_fusion = s32[128,16,16]{2,1,0:T(8,128)S(1)} fusion(s32[128,16,16]{2,1,0:T(8,128)S(1)} %convolution_minimum_fusion.2), kind=kOutput, calls=%fused_computation.10 | convolution fusion | flops 2162688 | bytes 262144 | tf_op jit(solution)/shard_map/rij,rjk->rik/dot_general | solution.py:23
  28.7 0.0 copy-start.1
  28.7 0.8 fusion.73
  29.6 56.3 %all-gather.9.cloned.1.call-done = bf16[128,16,1,256]{3,1,2,0:T(8,128)(2,1)} async-done(((bf16[4,16,1,256]{3,1,2,0:T(8,128)(2,1)}), bf16[128,16,1,256]{3,1,2,0:T(8,128)(2,1)}) %all-gather.9.cloned.1.call-update) | async-done | bytes 1048592 | tf_op jit(solution)/shard_map/all_gather | solution.py:65
  85.9 1.6 convolution_convert_fusion.1
  87.5 71.4 %all-gather.5.cloned.1.call-done = bf16[128,16,1024]{2,1,0:T(8,128)(2,1)} async-done(((bf16[4,16,1024]{2,1,0:T(8,128)(2,1)}), bf16[128,16,1024]{2,1,0:T(8,128)(2,1)}) %all-gather.5.cloned.1.call-update) | async-done | bytes 4194320 | tf_op jit(solution)/shard_map/all_gather | solution.py:64
  159.0 6.7 %fusion.13 = bf16[16,16,1024]{2,0,1:T(8,128)(2,1)S(1)} fusion(bf16[128,16,1024]{2,1,0:T(8,128)(2,1)} %all-gather.5.cloned.1.call-done, s32[128]{0:T(128)S(1)} %convert_reduce_fusion, pred[128]{0:T(512)(128)(4,1)S(1)} %get-tuple-element.12), kind=kOutput, calls=%fused_computation.19 | convolution fusion | flops 67375104 | bytes 4719232 | tf_op jit(solution)/shard_map/sr,rnk->snk/dot_general | solution.py:76
  165.6 0.1 copy.54
  165.7 0.5 fusion.74
  166.2 0.0 collective-permute-done
  166.2 0.0 copy-done.1
  166.3 3.4 multiply_reduce_fusion
  169.6 3.5 fusion
  173.1 0.7 fusion.27
  173.8 0.1 multiply_add_fusion
  173.9 1.1 convolution_multiply_fusion
  175.0 3.9 divide_convert_fusion
  178.9 1.0 convert_element_type.54
  179.9 0.0 all-gather.7.cloned.1.call-update
  179.9 0.0 reduce-scatter.2.cloned.1.call-start
  179.9 0.1 broadcast_in_dim.25
  180.0 0.1 broadcast_in_dim.26
  180.1 103.8 %all-gather.7.cloned.1.call-done = bf16[512,16,1024]{2,1,0:T(8,128)(2,1)} async-done(((bf16[16,16,1024]{2,1,0:T(8,128)(2,1)}), bf16[512,16,1024]{2,1,0:T(8,128)(2,1)}) %all-gather.7.cloned.1.call-update) | async-done | bytes 16777232 | tf_op jit(solution)/shard_map/all_gather | solution.py:111
  284.0 8.5 %gather_fusion = bf16[128,16,1024]{2,1,0:T(8,128)(2,1)} fusion(bf16[512,16,1024]{2,1,0:T(8,128)(2,1)} %all-gather.7.cloned.1.call-done, s32[1024]{0:T(1024)S(1)} %pad_clamp_fusion), kind=kCustom, calls=%fused_computation | custom fusion | bytes 8389120 | tf_op jit(solution)/shard_map/jit(_take)/gather | solution.py:112
  292.5 2.5 bitcast_select_fusion
  295.0 0.0 copy-done
  295.0 3.7 convolution_convert_fusion
  298.8 0.0 reduce-scatter.2.cloned.1.call-update
  298.8 85.7 %reduce-scatter.2.cloned.1.call-done = bf16[128,512]{1,0:T(8,128)(2,1)} async-done(((bf16[2048,512]{1,0:T(8,128)(2,1)}), bf16[128,512]{1,0:T(8,128)(2,1)}) %reduce-scatter.2.cloned.1.call-update) | async-done | bytes 131088 | tf_op jit(solution)/shard_map/reduce_scatter | solution.py:114
  (5 shorter events, 0.1 us)
Async XLA Ops:
  6.5 288.5 %copy-start = (bf16[1024,512]{1,0:T(8,128)(2,1)S(1)}, bf16[1024,512]{1,0:T(8,128)(2,1)}, u32[]{:S(2)}) copy-start(bf16[1024,512]{1,0:T(8,128)(2,1)} %param.11) | copy-start | bytes 3145732
  6.5 79.3 %all-gather.9.cloned.1.call-start = ((), (), s32[]{:S(2)}) async-start(), calls=%async_computation.4 | async-start | bytes 1081344 | tf_op jit(solution)/shard_map/all_gather | solution.py:65
  8.3 150.7 %all-gather.5.cloned.1.call-start = ((), (), s32[]{:S(2)}) async-start(), calls=%async_computation.1 | async-start | bytes 4325376 | tf_op jit(solution)/shard_map/all_gather | solution.py:64
  9.1 274.9 %all-gather.7.cloned.1.call-start = ((), (), s32[]{:S(2)}) async-start(), calls=%async_computation.2 | async-start | bytes 17301504 | tf_op jit(solution)/shard_map/all_gather | solution.py:111
  9.1 157.1 %collective-permute-start = (bf16[1024,256]{1,0:T(8,128)(2,1)}, bf16[1024,256]{1,0:T(8,128)(2,1)}, u32[]{:S(2)}, u32[]{:S(2)}) collective-permute-start(bf16[1024,256]{1,0:T(8,128)(2,1)} %bitcast.45), channel_id=1, source_target_pairs={{0,1},{1,0},{2,3},{3,2},{4,5},{5,4},{6,7},{7,6},{8,9},{9,8},{10,11... | collective-permute-start | bytes 1572872 | tf_op jit(solution)/shard_map/ppermute | solution.py:12
  28.7 137.5 %copy-start.1 = (bf16[1,1,1024,256]{3,2,1,0:T(8,128)(2,1)S(1)}, bf16[1,1,1024,256]{3,2,1,0:T(8,128)(2,1)}, u32[]{:S(2)}) copy-start(bf16[1,1,1024,256]{3,2,1,0:T(8,128)(2,1)} %param.8) | copy-start | bytes 1572868
  179.9 204.6 %reduce-scatter.2.cloned.1.call-start = ((), (), s32[]{:S(2)}) async-start(), calls=%async_computation.3 | async-start | bytes 2228224 | tf_op jit(solution)/shard_map/reduce_scatter | solution.py:114
Sparse Core Ops, SparseCore 0:
  9.5 76.3 all-gather.8
  88.0 70.9 all-gather.4
  180.0 103.8 all-gather.6
  298.9 85.5 reduce-scatter.1
where the time goes:
time: 392 us; the launch traced here: 391 us
  waiting for transfers between devices  318 us (81%)
  matrix products  34.8 us (9%)
  between operations  13.3 us (3%)
  local copies, waits for them, and re-layouts  12.4 us (3%)
  other arithmetic  8.35 us (2%)
  starting transfers between devices  4.16 us (1%)
    all_gather x1, waiting for transfers between devices, local(): every = lax.all_gather(attended, 'dp', axis=0, tiled=True)  104 us
    reduce_scatter x1, waiting for transfers between devices, local(): lax.psum_scatter(jnp.dot(flat, out_weight, preferred_element_type=jnp.flo...  85.7 us
    all_gather x1, waiting for transfers between devices, local(): lax.all_gather(queries, 'dp', axis=0, tiled=True)  71.4 us
    all_gather x1, waiting for transfers between devices, local(): lax.all_gather(tree_local, 'dp', axis=0, tiled=True)  56.3 us
    dot_general x2, matrix products, ancestors(): reach = jnp.minimum(jnp.einsum('rij,rjk->rik', reach, reach), 1)  13.2 us
    gather x1, local copies, waits for them, and re-layouts, local(): rows = jnp.take(every, request_holder * capacity + rank, axis=0)  8.52 us
  transfers between devices with their start and end apart: 5, of which 4 were waited for; matrix products, arithmetic and copies ran while one was open for 7% of the time, Pallas kernels for 0%

commit v1 on v0

v1 whole, which is shorter than its diff:
```python
import math

import jax
import jax.numpy as jnp
from jax import lax
from jax.experimental import pallas as pl
from jax.experimental.pallas import tpu as pltpu
from jax.sharding import PartitionSpec as P

CAP = 16
PAIR = 2
NEG = -1e30


def swapped(x, axis, bit):
    return lax.ppermute(x, axis, [(i, i ^ 1 << bit) for i in range(lax.axis_size(axis))])


def attend_kernel(index_ref, parent_ref, first_ref, second_ref, own_ref, other_ref, out_ref, reach_ref, value_ref):
    step = pl.program_id(0)
    nodes = first_ref.shape[1]
    width = own_ref.shape[1] // 2
    heads = (first_ref.shape[2] - 2 * width) // width
    half = own_ref.shape[0]
    rows = CAP * nodes

    @pl.when(step == 0)
    def _():
        line = lax.broadcasted_iota(jnp.int32, (rows, rows), 0)
        column = lax.broadcasted_iota(jnp.int32, (rows, rows), 1)
        above = (line // nodes) * nodes + parent_ref[...]
        reach = jnp.where((column == line) | (column == above), 1.0, 0.0).astype(jnp.bfloat16)
        for level in range(4):
            reach = jnp.minimum(
                jnp.dot(reach, reach, preferred_element_type=jnp.float32), 1.0
            ).astype(jnp.bfloat16)
        reach_ref[...] = reach.astype(jnp.float32)
        value_ref[pl.ds(0, half), :width] = own_ref[:, width:]
        value_ref[pl.ds(half, half), :width] = other_ref[:, width:]
        value_ref[:, width:] = jnp.ones((2 * half, width), jnp.bfloat16)

    scale = 1.0 / math.sqrt(width) * math.log2(math.e)
    refs = (first_ref, second_ref)
    query = jnp.concatenate(
        [ref[0, :, h * width : (h + 1) * width] for ref in refs for h in range(heads)], axis=0
    )
    tree = jnp.concatenate([ref[0, :, heads * width :] for ref in refs], axis=0)
    dims = (((1,), (1,)), ((), ()))
    near = lax.dot_general(query, own_ref[:, :width], dims, preferred_element_type=jnp.float32)
    far = lax.dot_general(query, other_ref[:, :width], dims, preferred_element_type=jnp.float32)
    drafts = lax.dot_general(query, tree[:, :width], dims, preferred_element_type=jnp.float32)
    span = PAIR * nodes
    mask = jnp.zeros((span, span), jnp.float32)
    for k in range(CAP // PAIR):
        block = reach_ref[k * span : (k + 1) * span, k * span : (k + 1) * span]
        mask = jnp.where(step == k, block, mask)
    mask = jnp.concatenate(
        [mask[s * nodes : (s + 1) * nodes] for s in range(PAIR) for h in range(heads)], axis=0
    )
    drafts = jnp.where(mask > 0, drafts, NEG)
    top = jnp.maximum(
        jnp.maximum(jnp.max(near, axis=1, keepdims=True), jnp.max(far, axis=1, keepdims=True)),
        jnp.max(drafts, axis=1, keepdims=True),
    )
    near = jnp.exp2((near - top) * scale).astype(jnp.bfloat16)
    far = jnp.exp2((far - top) * scale).astype(jnp.bfloat16)
    drafts = (jnp.exp2((drafts - top) * scale) * mask).astype(jnp.bfloat16)
    tree_value = jnp.concatenate([tree[:, width:], jnp.ones((span, width), jnp.bfloat16)], axis=1)
    summed = (
        jnp.dot(near, value_ref[pl.ds(0, half), :], preferred_element_type=jnp.float32)
        + jnp.dot(far, value_ref[pl.ds(half, half), :], preferred_element_type=jnp.float32)
        + jnp.dot(drafts, tree_value, preferred_element_type=jnp.float32)
    )
    attended = (summed[:, :width] / summed[:, width:]).astype(jnp.bfloat16)
    for s in range(PAIR):
        for h in range(heads):
            start = (s * heads + h) * nodes
            out_ref[s, :, h * width : (h + 1) * width] = attended[start : start + nodes]


def attend(index, parent, packed, own, other):
    nodes = packed.shape[1]
    depth = packed.shape[2]
    width = own.shape[1] // 2
    half = own.shape[0]
    model = depth - 2 * width
    return pl.pallas_call(
        attend_kernel,
        out_shape=jax.ShapeDtypeStruct((CAP, nodes, model), jnp.bfloat16),
        grid_spec=pltpu.PrefetchScalarGridSpec(
            num_scalar_prefetch=1,
            grid=(CAP // PAIR,),
            in_specs=[
                pl.BlockSpec((CAP * nodes, 1), lambda i, index: (0, 0)),
                pl.BlockSpec((1, nodes, depth), lambda i, index: (index[PAIR * i], 0, 0)),
                pl.BlockSpec((1, nodes, depth), lambda i, index: (index[PAIR * i + 1], 0, 0)),
                pl.BlockSpec((half, 2 * width), lambda i, index: (0, 0)),
                pl.BlockSpec((half, 2 * width), lambda i, index: (0, 0)),
            ],
            out_specs=pl.BlockSpec((PAIR, nodes, model), lambda i, index: (i, 0, 0)),
            scratch_shapes=[
                pltpu.VMEM((CAP * nodes, CAP * nodes), jnp.float32),
                pltpu.VMEM((2 * half, 2 * width), jnp.bfloat16),
            ],
        ),
        compiler_params=pltpu.CompilerParams(vmem_limit_bytes=40 * 1024 * 1024),
        name="attend",
    )(index, parent, packed, packed, own, other)


def project_kernel(place_ref, every_ref, weight_ref, out_ref, rows_ref, sems):
    lanes, depth = out_ref.shape[0], weight_ref.shape[0]
    requests, nodes = rows_ref.shape[0], rows_ref.shape[1]
    share = requests // lanes
    copies = []
    for r in range(requests):
        copy = pltpu.make_async_copy(every_ref.at[place_ref[r]], rows_ref.at[r], sems.at[r])
        copy.start()
        copies.append(copy)
    for lane in range(lanes):
        for copy in copies[lane * share : (lane + 1) * share]:
            copy.wait()
        block = rows_ref[lane * share : (lane + 1) * share].reshape(share * nodes, depth)
        out_ref[lane] = jnp.dot(
            block, weight_ref[...], preferred_element_type=jnp.float32
        ).astype(jnp.bfloat16)


def project(place, every, weight, lanes):
    requests = place.shape[0]
    nodes, depth = every.shape[1], every.shape[2]
    columns = weight.shape[1]
    return pl.pallas_call(
        project_kernel,
        out_shape=jax.ShapeDtypeStruct((lanes, requests // lanes * nodes, columns), jnp.bfloat16),
        grid_spec=pltpu.PrefetchScalarGridSpec(
            num_scalar_prefetch=1,
            grid=(),
            in_specs=[
                pl.BlockSpec(memory_space=pl.ANY),
                pl.BlockSpec(memory_space=pltpu.VMEM),
            ],
            out_specs=pl.BlockSpec(memory_space=pltpu.VMEM),
            scratch_shapes=[
                pltpu.VMEM((requests, nodes, depth), jnp.bfloat16),
                pltpu.SemaphoreType.DMA((requests,)),
            ],
        ),
        compiler_params=pltpu.CompilerParams(vmem_limit_bytes=40 * 1024 * 1024),
        name="project",
    )(place, every, weight)


def local(queries, tree_kv, prefix_kv, request_holder, parents, out_weight):
    group = lax.axis_index("dp")
    lane = lax.axis_index("tensor")
    lanes = lax.axis_size("tensor")
    requests = request_holder.shape[0]
    nodes = queries.shape[1]
    tree_local = lax.dynamic_index_in_dim(tree_kv, lane // 2, 2, keepdims=False)
    packed = lax.all_gather(
        jnp.concatenate([queries, tree_local], axis=2), "dp", axis=0, tiled=True
    )
    own_half = prefix_kv[0, 0]
    other_half = swapped(own_half, "tensor", 0)
    order = jnp.arange(requests, dtype=jnp.int32)
    same = request_holder[:, None] == request_holder[None, :]
    rank = jnp.sum((same & (order[None, :] < order[:, None])).astype(jnp.int32), axis=1)
    slots = jnp.arange(CAP, dtype=jnp.int32)
    pick = ((request_holder[None, :] == group) & (rank[None, :] == slots[:, None])).astype(jnp.int32)
    index = jnp.sum(pick * order[None, :], axis=1)
    slot_parents = jnp.sum(pick[:, :, None] * parents[None], axis=1).reshape(CAP * nodes, 1)
    attended = attend(index, slot_parents, packed, own_half, other_half)
    every = lax.all_gather(attended, "dp", axis=0, tiled=True)
    partial = project(request_holder * CAP + rank, every, out_weight, lanes)
    shares = lax.all_to_all(partial, "tensor", 0, 0, tiled=True)
    total = jnp.sum(shares.astype(jnp.float32), axis=0).astype(jnp.bfloat16)
    return total.reshape(requests // lanes, nodes, out_weight.shape[1])


def solution(mesh):
    return jax.shard_map(
        local,
        mesh=mesh,
        in_specs=(
            P("dp", None, "tensor"),
            P("dp", None, None, None),
            P("dp", "tensor", None, None),
            P(),
            P(),
            P("tensor", "dp"),
        ),
        out_specs=P("tensor", None, "dp"),
        check_vma=False,
    )
```

time: 392 us -> 263 us (0.67)
  waiting for transfers between devices: 318 us -> 178 us
  matrix products: 34.8 us -> 0 us
  blocking collectives: 0 us -> 33.5 us
  Pallas kernels: 0 us -> 22.9 us
  local copies, waits for them, and re-layouts: 12.4 us -> 4.67 us
    reduce_scatter x1 -> x0, waiting for transfers between devices: 85.7 us -> none  [local(): lax.psum_scatter(jnp.dot(flat, out_weight, preferred_element_type=jnp.flo...]
    all_gather x2 -> x1, waiting for transfers between devices: 128 us -> 70.7 us  [local(): lax.all_gather(jnp.concatenate([queries, tree_local], axis=2), 'dp', axis...]
    dot_general x10 -> x0, matrix products: 34.8 us -> none  [the longest x2 13.2 us: ancestors(): reach = jnp.minimum(jnp.einsum('rij,rjk->rik', reach, reach), 1)]
    all_to_all x0 -> x1, blocking collectives: none -> 33.5 us  [local(): shares = lax.all_to_all(partial, 'tensor', 0, 0, tiled=True)]
    pallas_call x0 -> x2, Pallas kernels: none -> 22.9 us  [the longest x1 15.1 us: attend(): pl.pallas_call(attend_kernel, out_shape=jax.ShapeDtypeStruct((CAP, nodes,...]
    gather x1 -> x0, local copies, waits for them, and re-layouts: 8.52 us -> none  [local(): rows = jnp.take(every, request_holder * capacity + rank, axis=0)]
    ppermute x1, waiting for transfers between devices: 0.01 us -> 4.15 us  [swapped(): lax.ppermute(x, axis, [(i, i ^ 1 << bit) for i in range(lax.axis_size(axi...]
  transfers between devices with their start and end apart: 5 -> 3, of which waited for: 4 -> 3; matrix products, arithmetic and copies ran while one was open for 7% -> 1% of each run, Pallas kernels for 0% -> 0%
where the time goes in v1:
time: 263 us; the launch traced here: 262 us
  waiting for transfers between devices  178 us (68%)
  blocking collectives  33.5 us (13%)
  Pallas kernels  22.9 us (9%)
  between operations  13.5 us (5%)
  other arithmetic  5.28 us (2%)
  local copies, waits for them, and re-layouts  4.67 us (2%)
  starting transfers between devices  4.08 us (2%)
    all_gather x1, waiting for transfers between devices, local(): every = lax.all_gather(attended, 'dp', axis=0, tiled=True)  103 us
    all_gather x1, waiting for transfers between devices, local(): lax.all_gather(jnp.concatenate([queries, tree_local], axis=2), 'dp', axis...  70.7 us
    all_to_all x1, blocking collectives, local(): shares = lax.all_to_all(partial, 'tensor', 0, 0, tiled=True)  33.5 us
    pallas_call x1, Pallas kernels, attend(): pl.pallas_call(attend_kernel, out_shape=jax.ShapeDtypeStruct((CAP, nodes,...  15.1 us
    pallas_call x1, Pallas kernels, project(): pl.pallas_call(project_kernel, out_shape=jax.ShapeDtypeStruct((lanes, req...  7.8 us
  transfers between devices with their start and end apart: 3, of which 3 were waited for; matrix products, arithmetic and copies ran while one was open for 1% of the time, Pallas kernels for 0%

profile of v1, /device:TPU:1, one launch (start us, length us, event | category | flops | bytes accessed | tf_op | source)
XLA Modules:
  0.0 262.2 jit_solution(15872336621650682093)
XLA Ops:
  6.5 0.0 copy-start
  6.5 0.0 all-gather.3.cloned.1.call-start
  6.5 0.9 copy-done
  7.5 0.1 constant_dynamic-slice_fusion
  7.6 1.6 pad_maximum_fusion
  9.2 0.0 all-gather.3.cloned.1.call-update
  9.2 0.0 all-gather.5.cloned.1.call-start
  9.2 4.0 %collective-permute-start = (bf16[1024,256]{1,0:T(8,128)(2,1)}, bf16[1024,256]{1,0:T(8,128)(2,1)S(1)}, u32[]{:S(2)}, u32[]{:S(2)}) collective-permute-start(bf16[1024,256]{1,0:T(8,128)(2,1)} %bitcast.5), channel_id=1, source_target_pairs={{0,1},{1,0},{2,3},{3,2},{4,5},{5,4},{6,7},{7,6},{8,9},{9,8},{10,11... | collective-permute-start | bytes 1572872 | tf_op jit(solution)/shard_map/ppermute | solution.py:16
  13.3 0.7 broadcast_compare_fusion
  13.9 0.9 convert_reduce_fusion
  14.9 1.0 multiply_reduce_fusion
  15.9 0.1 reshape.41.parent_ref
  16.0 0.0 copy-start.4
  16.0 0.1 select_reduce_fusion.index_ref
  16.2 4.2 %collective-permute-done.other_ref = bf16[1024,256]{1,0:T(8,128)(2,1)S(1)} collective-permute-done((bf16[1024,256]{1,0:T(8,128)(2,1)}, bf16[1024,256]{1,0:T(8,128)(2,1)S(1)}, u32[]{:S(2)}, u32[]{:S(2)}) %collective-permute-start) | collective-permute-done | bytes 524320 | tf_op jit(solution)/shard_map/ppermute | solution.py:16
  20.3 70.7 %all-gather.3.cloned.1.call-done.first_ref.second_ref = bf16[128,16,1280]{2,1,0:T(8,128)(2,1)} async-done(((bf16[4,16,1280]{2,1,0:T(8,128)(2,1)}), bf16[128,16,1280]{2,1,0:T(8,128)(2,1)}) %all-gather.3.cloned.1.call-update) | async-done | bytes 5242896 | tf_op jit(solution)/shard_map/all_gather | solution.py:161
  91.0 0.0 copy-start.1
  91.0 2.5 copy-done.1
  93.5 0.0 copy-start.3
  93.5 1.0 copy-done.3
  94.5 0.0 copy-start.2
  94.5 15.1 %attend.1 = bf16[16,16,1024]{2,1,0:T(8,128)(2,1)} custom-call(s32[16]{0:T(128)S(1)} %select_reduce_fusion.index_ref, s32[256,1]{1,0:T(8,128)S(1)} %reshape.41.parent_ref, bf16[128,16,1280]{2,1,0:T(8,128)(2,1)S(1)} %copy-done.1, bf16[128,16,1280]{2,1,0:T(8,128)(2,1)S(1)} %copy-done.1, bf16[1024,256]{1,0:T(8,128)(2,1)S(1)} %bitcast.6, ...), custom_call_target="tpu_custom_call" | custom-call | tf_op jit(solution)/shard_map/attend/pallas_call | solution.py:87
  109.6 0.0 all-gather.5.cloned.1.call-update
  109.6 0.0 copy-done.4
  109.6 103.4 %all-gather.5.cloned.1.call-done.every_ref = bf16[512,16,1024]{2,1,0:T(8,128)(2,1)} async-done(((bf16[16,16,1024]{2,1,0:T(8,128)(2,1)}), bf16[512,16,1024]{2,1,0:T(8,128)(2,1)}) %all-gather.5.cloned.1.call-update) | async-done | bytes 16777232 | tf_op jit(solution)/shard_map/all_gather | solution.py:174
  213.1 0.0 copy-done.2
  213.1 7.8 %project.1 = bf16[16,128,512]{2,1,0:T(8,128)(2,1)S(1)} custom-call(s32[128]{0:T(128)S(1)} %multiply_add_fusion.place_ref, bf16[512,16,1024]{2,1,0:T(8,128)(2,1)} %all-gather.5.cloned.1.call-done.every_ref, bf16[1024,512]{1,0:T(8,128)(2,1)S(1)} %copy-done.2), custom_call_target="tpu_custom_call" | custom-call | tf_op jit(solution)/shard_map/project/pallas_call | solution.py:133
  220.9 33.5 %all_to_all.5 = bf16[16,128,512]{2,1,0:T(8,128)(2,1)S(1)} all-to-all(bf16[16,128,512]{2,1,0:T(8,128)(2,1)S(1)} %project.1), channel_id=1, replica_groups=mesh['dp'=32,'tensor'=16] {'tensor'}, dimensions={0} | all-to-all | bytes 4194304 | tf_op jit(solution)/shard_map/all_to_all | solution.py:176
  254.4 1.0 reduce_sum.42
  (3 shorter events, 0.0 us)
Async XLA Ops:
  6.5 1.0 copy-start
  6.5 84.4 %all-gather.3.cloned.1.call-start = ((), (), s32[]{:S(2)}) async-start(), calls=%async_computation.1 | async-start | bytes 5406720 | tf_op jit(solution)/shard_map/all_gather | solution.py:161
  9.2 203.9 %all-gather.5.cloned.1.call-start = ((), (), s32[]{:S(2)}) async-start(), calls=%async_computation.2 | async-start | bytes 17301504 | tf_op jit(solution)/shard_map/all_gather | solution.py:174
  9.2 11.1 %collective-permute-start = (bf16[1024,256]{1,0:T(8,128)(2,1)}, bf16[1024,256]{1,0:T(8,128)(2,1)S(1)}, u32[]{:S(2)}, u32[]{:S(2)}) collective-permute-start(bf16[1024,256]{1,0:T(8,128)(2,1)} %bitcast.5), channel_id=1, source_target_pairs={{0,1},{1,0},{2,3},{3,2},{4,5},{5,4},{6,7},{7,6},{8,9},{9,8},{10,11... | collective-permute-start | bytes 1572872 | tf_op jit(solution)/shard_map/ppermute | solution.py:16
  16.0 93.6 %copy-start.4 = (s32[128]{0:T(128)S(1)}, s32[128]{0:T(128)}, u32[]{:S(2)}) copy-start(s32[128]{0:T(128)} %param.9) | copy-start | bytes 1540
  91.0 2.5 copy-start.1
  93.5 1.0 copy-start.3
  94.5 118.5 %copy-start.2 = (bf16[1024,512]{1,0:T(8,128)(2,1)S(1)}, bf16[1024,512]{1,0:T(8,128)(2,1)}, u32[]{:S(2)}) copy-start(bf16[1024,512]{1,0:T(8,128)(2,1)} %weight_ref.1) | copy-start | bytes 3145732
Sparse Core Ops, SparseCore 0:
  9.5 81.4 all-gather.2
  109.7 103.2 all-gather.4

commit v2 on v1

v2 whole, which is shorter than its diff:
```python
import math

import jax
import jax.numpy as jnp
from jax import lax
from jax.experimental import pallas as pl
from jax.experimental.pallas import tpu as pltpu
from jax.sharding import PartitionSpec as P

CAP = 16
PAIR = 2
NEG = -1e30
RAISE = 2.0**11


def swapped(x, axis, bit):
    return lax.ppermute(x, axis, [(i, i ^ 1 << bit) for i in range(lax.axis_size(axis))])


def exponent(x):
    peak = jnp.max(jnp.abs(x), axis=-1, keepdims=True)
    return jnp.floor(jnp.log2(jnp.clip(peak, 2.0**-100, 2.0**6)))


def pack_kernel(place_ref, queries_ref, tree_ref, holder_ref, packed_ref, slot_ref, index_ref, place_out_ref):
    group, column = place_ref[0], place_ref[1]
    count, nodes, model = queries_ref.shape
    kv_heads, width = tree_ref.shape[2], tree_ref.shape[3] // 2
    pick = lax.broadcasted_iota(jnp.int32, (nodes, kv_heads, 2 * width), 1) == column
    for r in range(count):
        packed_ref[r, :, :model] = (queries_ref[r].astype(jnp.float32) * RAISE).astype(jnp.bfloat16)
        tree = jnp.sum(jnp.where(pick, tree_ref[r].astype(jnp.float32), 0.0), axis=1)
        packed_ref[r, :, model : model + width] = (tree[:, :width] * RAISE).astype(jnp.bfloat16)
        values = tree[:, width:]
        power = exponent(values)
        packed_ref[r, :, model + width : model + 2 * width] = (
            values * jnp.exp2(10.0 - power)
        ).astype(jnp.bfloat16)
        packed_ref[r, :, model + 2 * width :] = jnp.broadcast_to(power, values.shape).astype(
            jnp.bfloat16
        )
    requests = holder_ref.shape[1]
    line = lax.broadcasted_iota(jnp.int32, (requests, requests), 0)
    lane = lax.broadcasted_iota(jnp.int32, (requests, requests), 1)
    row = holder_ref[...]
    rows = jnp.broadcast_to(row, (requests, requests))
    column = jnp.sum(jnp.where(line == lane, rows, 0), axis=1, keepdims=True)
    before = jnp.where((column == rows) & (line < lane), 1, 0)
    rank = jnp.sum(before, axis=0, keepdims=True)
    after = jnp.where((column == rows) & (lane < line), 1, 0)
    rank_column = jnp.sum(after, axis=1, keepdims=True)
    slot_ref[...] = jnp.where(row == group, rank, -1)
    place_out_ref[...] = row * CAP + rank
    mine = (column == group) & (rank_column == lane)
    index_ref[...] = jnp.sum(jnp.where(mine, line, 0), axis=0, keepdims=True)


def pack(place, queries, tree, holder):
    count, nodes, model = queries.shape
    width = tree.shape[3] // 2
    requests = holder.shape[0]
    vmem = pl.BlockSpec(memory_space=pltpu.VMEM)
    line = jax.ShapeDtypeStruct((1, requests), jnp.int32)
    return pl.pallas_call(
        pack_kernel,
        out_shape=(
            jax.ShapeDtypeStruct((count, nodes, model + 3 * width), jnp.bfloat16),
            line,
            line,
            line,
        ),
        grid_spec=pltpu.PrefetchScalarGridSpec(
            num_scalar_prefetch=1, grid=(), in_specs=[vmem] * 3, out_specs=(vmem,) * 4
        ),
        compiler_params=pltpu.CompilerParams(vmem_limit_bytes=40 * 1024 * 1024),
        name="pack",
    )(place, queries, tree, holder.reshape(1, requests))


def attend_kernel(slot_ref, parents_ref, picked_ref, own_ref, other_ref, out_ref, reach_ref, value_ref):
    step = pl.program_id(0)
    nodes = picked_ref.shape[1]
    width = own_ref.shape[1] // 2
    heads = (picked_ref.shape[2] - 3 * width) // width
    half = own_ref.shape[0]
    rows = CAP * nodes

    @pl.when(step == 0)
    def _():
        line = lax.broadcasted_iota(jnp.int32, (rows, rows), 0)
        column = lax.broadcasted_iota(jnp.int32, (rows, rows), 1)
        requests = slot_ref.shape[1]
        taken = lax.broadcasted_iota(jnp.int32, (rows, requests), 0) // nodes == slot_ref[...]
        above = jnp.dot(
            jnp.where(taken, 1.0, 0.0).astype(jnp.bfloat16),
            parents_ref[...].astype(jnp.float32).astype(jnp.bfloat16),
            preferred_element_type=jnp.float32,
        )
        node = lax.broadcasted_iota(jnp.int32, (rows, nodes), 0) % nodes
        own_node = lax.broadcasted_iota(jnp.int32, (rows, nodes), 1) == node
        above = jnp.sum(jnp.where(own_node, above, 0.0), axis=1, keepdims=True).astype(jnp.int32)
        above = (line // nodes) * nodes + above
        reach = jnp.where((column == line) | (column == above), 1.0, 0.0).astype(jnp.bfloat16)
        for level in range(4):
            reach = jnp.minimum(
                jnp.dot(reach, reach, preferred_element_type=jnp.float32), 1.0
            ).astype(jnp.bfloat16)
        reach_ref[...] = reach.astype(jnp.float32)
        value_ref[pl.ds(0, half), :width] = own_ref[:, width:]
        value_ref[pl.ds(half, half), :width] = other_ref[:, width:]
        value_ref[:, width:] = jnp.ones((2 * half, width), jnp.bfloat16)

    scale = 1.0 / math.sqrt(width) * math.log2(math.e) / RAISE
    query = jnp.concatenate(
        [picked_ref[s, :, h * width : (h + 1) * width] for s in range(PAIR) for h in range(heads)],
        axis=0,
    )
    tree = jnp.concatenate([picked_ref[s, :, heads * width :] for s in range(PAIR)], axis=0)
    dims = (((1,), (1,)), ((), ()))
    span = PAIR * nodes
    mask = jnp.zeros((span, span), jnp.float32)
    for k in range(CAP // PAIR):
        block = reach_ref[k * span : (k + 1) * span, k * span : (k + 1) * span]
        mask = jnp.where(step == k, block, mask)
    mask = jnp.concatenate(
        [mask[s * nodes : (s + 1) * nodes] for s in range(PAIR) for h in range(heads)], axis=0
    )
    drafts = lax.dot_general(query, tree[:, :width], dims, preferred_element_type=jnp.float32)
    drafts = jnp.where(mask > 0, drafts * (1.0 / RAISE), NEG)
    peak = jnp.max(drafts, axis=1, keepdims=True)
    drafts = (jnp.exp2((drafts - peak) * scale) * mask).astype(jnp.bfloat16)
    power = tree[:, 2 * width :].astype(jnp.float32) - 10.0
    tree_value = (tree[:, width : 2 * width].astype(jnp.float32) * jnp.exp2(power)).astype(
        jnp.bfloat16
    )
    tree_value = jnp.concatenate([tree_value, jnp.ones((span, width), jnp.bfloat16)], axis=1)
    peaks = [peak]
    sums = [jnp.dot(drafts, tree_value, preferred_element_type=jnp.float32)]
    for k, ref in enumerate((own_ref, other_ref)):
        scores = lax.dot_general(query, ref[:, :width], dims, preferred_element_type=jnp.float32)
        peak = jnp.max(scores, axis=1, keepdims=True)
        weights = jnp.exp2((scores - peak) * scale).astype(jnp.bfloat16)
        peaks.append(peak)
        sums.append(
            jnp.dot(
                weights, value_ref[pl.ds(k * half, half), :], preferred_element_type=jnp.float32
            )
        )
    top = jnp.maximum(jnp.maximum(peaks[0], peaks[1]), peaks[2])
    summed = sum(jnp.exp2((peak - top) * scale) * part for peak, part in zip(peaks, sums))
    attended = (summed[:, :width] / summed[:, width:]).astype(jnp.bfloat16)
    for s in range(PAIR):
        for h in range(heads):
            start = (s * heads + h) * nodes
            out_ref[s, :, h * width : (h + 1) * width] = attended[start : start + nodes]


def attend(slot, parents, picked, own, other):
    nodes = picked.shape[1]
    depth = picked.shape[2]
    width = own.shape[1] // 2
    half = own.shape[0]
    model = depth - 3 * width
    return pl.pallas_call(
        attend_kernel,
        out_shape=jax.ShapeDtypeStruct((CAP, nodes, model), jnp.bfloat16),
        grid=(CAP // PAIR,),
        in_specs=[
            pl.BlockSpec(slot.shape, lambda i: (0, 0)),
            pl.BlockSpec(parents.shape, lambda i: (0, 0)),
            pl.BlockSpec((PAIR, nodes, depth), lambda i: (i, 0, 0)),
            pl.BlockSpec((half, 2 * width), lambda i: (0, 0)),
            pl.BlockSpec((half, 2 * width), lambda i: (0, 0)),
        ],
        out_specs=pl.BlockSpec((PAIR, nodes, model), lambda i: (i, 0, 0)),
        scratch_shapes=[
            pltpu.VMEM((CAP * nodes, CAP * nodes), jnp.float32),
            pltpu.VMEM((2 * half, 2 * width), jnp.bfloat16),
        ],
        compiler_params=pltpu.CompilerParams(vmem_limit_bytes=40 * 1024 * 1024),
        name="attend",
    )(slot, parents, picked, own, other)


def project_kernel(place_ref, every_ref, weight_ref, out_ref, rows_ref, sems):
    lanes, depth = out_ref.shape[0], weight_ref.shape[0]
    requests, nodes = rows_ref.shape[0], rows_ref.shape[1]
    share = requests // lanes
    copies = []
    for r in range(requests):
        copy = pltpu.make_async_copy(every_ref.at[place_ref[0, r]], rows_ref.at[r], sems.at[r])
        copy.start()
        copies.append(copy)
    for lane in range(lanes):
        for copy in copies[lane * share : (lane + 1) * share]:
            copy.wait()
        block = rows_ref[lane * share : (lane + 1) * share].reshape(share * nodes, depth)
        out_ref[lane] = jnp.dot(
            block, weight_ref[...], preferred_element_type=jnp.float32
        ).astype(jnp.bfloat16)


def project(place, every, weight, lanes):
    requests = place.shape[1]
    nodes, depth = every.shape[1], every.shape[2]
    columns = weight.shape[1]
    return pl.pallas_call(
        project_kernel,
        out_shape=jax.ShapeDtypeStruct((lanes, requests // lanes * nodes, columns), jnp.bfloat16),
        grid_spec=pltpu.PrefetchScalarGridSpec(
            num_scalar_prefetch=1,
            grid=(),
            in_specs=[
                pl.BlockSpec(memory_space=pl.ANY),
                pl.BlockSpec(memory_space=pltpu.VMEM),
            ],
            out_specs=pl.BlockSpec(memory_space=pltpu.VMEM),
            scratch_shapes=[
                pltpu.VMEM((requests, nodes, depth), jnp.bfloat16),
                pltpu.SemaphoreType.DMA((requests,)),
            ],
        ),
        compiler_params=pltpu.CompilerParams(vmem_limit_bytes=40 * 1024 * 1024),
        name="project",
    )(place, every, weight)


def local(queries, tree_kv, prefix_kv, request_holder, parents, out_weight):
    group = lax.axis_index("dp")
    lane = lax.axis_index("tensor")
    lanes = lax.axis_size("tensor")
    requests = request_holder.shape[0]
    nodes = queries.shape[1]
    own_half = prefix_kv[0, 0]
    other_half = swapped(own_half, "tensor", 0)
    here = jnp.stack([group, lane // 2]).astype(jnp.int32)
    packed, slot, index, place = pack(here, queries, tree_kv, request_holder)
    packed = lax.all_gather(packed.astype(jnp.float16), "dp", axis=0, tiled=True)
    picked = packed.at[index[0, :CAP]].get(mode="promise_in_bounds").astype(jnp.bfloat16)
    attended = attend(slot, parents, picked, own_half, other_half)
    every = lax.all_gather(attended, "dp", axis=0, tiled=True)
    partial = project(place, every, out_weight, lanes)
    shares = lax.all_to_all(partial, "tensor", 0, 0, tiled=True)
    total = jnp.sum(shares.astype(jnp.float32), axis=0).astype(jnp.bfloat16)
    return total.reshape(requests // lanes, nodes, out_weight.shape[1])


def solution(mesh):
    return jax.shard_map(
        local,
        mesh=mesh,
        in_specs=(
            P("dp", None, "tensor"),
            P("dp", None, None, None),
            P("dp", "tensor", None, None),
            P(),
            P(),
            P("tensor", "dp"),
        ),
        out_specs=P("tensor", None, "dp"),
        check_vma=False,
    )
```

time: 263 us -> 244 us (0.928)
  waiting for transfers between devices: 178 us -> 103 us
  blocking collectives: 33.5 us -> 91.2 us
  other arithmetic: 5.28 us -> 1.17 us
    all_gather x1 -> x0, waiting for transfers between devices: 70.7 us -> none  [local(): lax.all_gather(jnp.concatenate([queries, tree_local], axis=2), 'dp', axis...]
    all_gather x0 -> x1, blocking collectives: none -> 57.7 us  [local(): lax.all_gather(packed.astype(jnp.float16), 'dp', axis=0, tiled=True)]
    ppermute x1, waiting for transfers between devices: 4.15 us -> 0.01 us  [swapped(): lax.ppermute(x, axis, [(i, i ^ 1 << bit) for i in range(lax.axis_size(axi...]
    gather x0 -> x1, local copies, waits for them, and re-layouts: none -> 3.5 us  [local(): packed.at[index[0, :CAP]].get(mode='promise_in_bounds').astype(jnp.bfloat16)]
  transfers between devices with their start and end apart: 3 -> 2, of which waited for: 3 -> 1; matrix products, arithmetic and copies ran while one was open for 1% -> 2% of each run, Pallas kernels for 0% -> 0%
where the time goes in v2:
time: 244 us
  waiting for transfers between devices  103 us (42%)
  blocking collectives  91.2 us (37%)
  Pallas kernels  24.6 us (10%)
  between operations  13.5 us (6%)
  local copies, waits for them, and re-layouts  6.12 us (3%)
  starting transfers between devices  4.16 us (2%)
    all_gather x1, waiting for transfers between devices, local(): every = lax.all_gather(attended, 'dp', axis=0, tiled=True)  103 us
    all_gather x1, blocking collectives, local(): lax.all_gather(packed.astype(jnp.float16), 'dp', axis=0, tiled=True)  57.7 us
    all_to_all x1, blocking collectives, local(): shares = lax.all_to_all(partial, 'tensor', 0, 0, tiled=True)  33.5 us
    pallas_call x1, Pallas kernels, attend(): pl.pallas_call(attend_kernel, out_shape=jax.ShapeDtypeStruct((CAP, nodes,...  15.8 us
    pallas_call x1, Pallas kernels, project(): pl.pallas_call(project_kernel, out_shape=jax.ShapeDtypeStruct((lanes, req...  7.86 us
  transfers between devices with their start and end apart: 2, of which 1 were waited for; matrix products, arithmetic and copies ran while one was open for 2% of the time, Pallas kernels for 0%

profile of v2, /device:TPU:1, one launch (start us, length us, event | category | flops | bytes accessed | tf_op | source)
XLA Modules:
  0.0 243.7 jit_solution(4857158300847973059)
XLA Ops:
  6.5 0.0 copy-start.1
  6.5 0.0 all-gather.3.cloned.1.call-start
  6.5 4.2 %collective-permute-start = (bf16[1024,256]{1,0:T(8,128)(2,1)}, bf16[1024,256]{1,0:T(8,128)(2,1)S(1)}, u32[]{:S(2)}, u32[]{:S(2)}) collective-permute-start(bf16[1024,256]{1,0:T(8,128)(2,1)} %bitcast.9), channel_id=1, source_target_pairs={{0,1},{1,0},{2,3},{3,2},{4,5},{5,4},{6,7},{7,6},{8,9},{9,8},{10,11... | collective-permute-start | bytes 1572872 | tf_op jit(solution)/shard_map/ppermute | solution.py:17
  10.7 0.1 pad_add_fusion.place_ref
  10.8 0.0 copy-start.2
  10.8 0.9 copy-done.2
  11.7 0.0 copy-start.3
  11.7 0.9 copy-done.3
  12.6 0.0 copy-start.4
  12.6 0.7 copy-done.4
  13.3 0.0 copy-start.5
  13.3 0.9 pack.1
  14.2 0.0 copy-start
  14.2 57.7 %all-gather.4 = f16[128,16,1408]{2,1,0:T(8,128)(2,1)} all-gather(f16[4,16,1408]{2,1,0:T(8,128)(2,1)S(1)} %convert_element_type.8), channel_id=1, replica_groups=mesh['dp'=32,'tensor'=16] {'dp'}, dimensions={0}, use_global_device_ids=true | all-gather | bytes 5947392 | tf_op jit(solution)/shard_map/all_gather | solution.py:238
  71.9 0.0 copy-done.5
  71.9 0.1 copy.8.parents_ref
  72.1 3.5 %gather_fusion = f16[16,16,1408]{2,1,0:T(8,128)(2,1)S(1)} fusion(f16[128,16,1408]{2,1,0:T(8,128)(2,1)} %all-gather.4, s32[1024]{0:T(1024)S(1)} %pad_clamp_fusion), kind=kCustom, calls=%fused_computation | custom fusion | bytes 1441856 | tf_op jit(solution)/shard_map/gather | solution.py:239
  75.6 0.1 convert_element_type.9.picked_ref
  75.7 0.0 collective-permute-done.other_ref
  75.7 0.0 copy-done.1
  75.7 15.8 %attend.1 = bf16[16,16,1024]{2,1,0:T(8,128)(2,1)} custom-call(s32[1,128]{1,0:T(1,128)S(1)} %get-tuple-element.10.slot_ref, s32[128,16]{1,0:T(8,128)S(1)} %copy.8.parents_ref, bf16[16,16,1408]{2,1,0:T(8,128)(2,1)S(1)} %convert_element_type.9.picked_ref, bf16[1024,256]{1,0:T(8,128)(2,1)S(1)} %bitcast.10, bf16[1024,256]{1,0:T(8,128)(2,1)S(1)} %collective-permute-done.other_ref), custom_call_target="tpu_custom_call" | custom-call | tf_op jit(solution)/shard_map/attend/pallas_call | solution.py:164
  91.5 0.0 all-gather.3.cloned.1.call-update
  91.6 102.9 %all-gather.3.cloned.1.call-done.every_ref = bf16[512,16,1024]{2,1,0:T(8,128)(2,1)} async-done(((bf16[16,16,1024]{2,1,0:T(8,128)(2,1)}), bf16[512,16,1024]{2,1,0:T(8,128)(2,1)}) %all-gather.3.cloned.1.call-update) | async-done | bytes 16777232 | tf_op jit(solution)/shard_map/all_gather | solution.py:241
  194.5 0.0 copy-done
  194.5 7.9 %project.1 = bf16[16,128,512]{2,1,0:T(8,128)(2,1)S(1)} custom-call(s32[1,128]{1,0:T(1,128)S(1)} %get-tuple-element.9.place_ref, bf16[512,16,1024]{2,1,0:T(8,128)(2,1)} %all-gather.3.cloned.1.call-done.every_ref, bf16[1024,512]{1,0:T(8,128)(2,1)S(1)} %copy-done), custom_call_target="tpu_custom_call" | custom-call | tf_op jit(solution)/shard_map/project/pallas_call | solution.py:207
  202.3 33.5 %all_to_all.5 = bf16[16,128,512]{2,1,0:T(8,128)(2,1)S(1)} all-to-all(bf16[16,128,512]{2,1,0:T(8,128)(2,1)S(1)} %project.1), channel_id=1, replica_groups=mesh['dp'=32,'tensor'=16] {'tensor'}, dimensions={0} | all-to-all | bytes 4194304 | tf_op jit(solution)/shard_map/all_to_all | solution.py:243
  235.9 1.0 reduce_sum.12
  (3 shorter events, 0.0 us)
Async XLA Ops:
  6.5 69.1 %copy-start.1 = (bf16[1,1,1024,256]{3,2,1,0:T(8,128)(2,1)S(1)}, bf16[1,1,1024,256]{3,2,1,0:T(8,128)(2,1)}, u32[]{:S(2)}) copy-start(bf16[1,1,1024,256]{3,2,1,0:T(8,128)(2,1)} %param.8) | copy-start | bytes 1572868
  6.5 187.9 %all-gather.3.cloned.1.call-start = ((), (), s32[]{:S(2)}) async-start(), calls=%async_computation.1 | async-start | bytes 17301504 | tf_op jit(solution)/shard_map/all_gather | solution.py:241
  6.5 69.1 %collective-permute-start = (bf16[1024,256]{1,0:T(8,128)(2,1)}, bf16[1024,256]{1,0:T(8,128)(2,1)S(1)}, u32[]{:S(2)}, u32[]{:S(2)}) collective-permute-start(bf16[1024,256]{1,0:T(8,128)(2,1)} %bitcast.9), channel_id=1, source_target_pairs={{0,1},{1,0},{2,3},{3,2},{4,5},{5,4},{6,7},{7,6},{8,9},{9,8},{10,11... | collective-permute-start | bytes 1572872 | tf_op jit(solution)/shard_map/ppermute | solution.py:17
  10.8 1.0 copy-start.2
  11.7 0.9 copy-start.3
  12.6 0.7 copy-start.4
  13.3 58.6 %copy-start.5 = (s32[128,16]{0,1:T(8,128)S(1)}, s32[128,16]{0,1:T(8,128)}, u32[]{:S(2)}) copy-start(s32[128,16]{0,1:T(8,128)} %param.10) | copy-start | bytes 24580
  14.2 180.3 %copy-start = (bf16[1024,512]{1,0:T(8,128)(2,1)S(1)}, bf16[1024,512]{1,0:T(8,128)(2,1)}, u32[]{:S(2)}) copy-start(bf16[1024,512]{1,0:T(8,128)(2,1)} %weight_ref.1) | copy-start | bytes 3145732
Sparse Core Ops, SparseCore 0:
  91.7 102.7 all-gather.2

commit v3 on v2

--- a/solution.py
+++ b/solution.py
@@ -8,7 +8,7 @@
 from jax.sharding import PartitionSpec as P
 
 CAP = 16
-PAIR = 2
+PAIR = 8
 NEG = -1e30
 RAISE = 2.0**11
 
@@ -22,7 +22,7 @@
     return jnp.floor(jnp.log2(jnp.clip(peak, 2.0**-100, 2.0**6)))
 
 
-def pack_kernel(place_ref, queries_ref, tree_ref, holder_ref, packed_ref, slot_ref, index_ref, place_out_ref):
+def pack_kernel(place_ref, queries_ref, tree_ref, holder_ref, packed_ref, slot_ref, index_ref, spot_ref, source_ref):
     group, column = place_ref[0], place_ref[1]
     count, nodes, model = queries_ref.shape
     kv_heads, width = tree_ref.shape[2], tree_ref.shape[3] // 2
@@ -45,14 +45,20 @@
     row = holder_ref[...]
     rows = jnp.broadcast_to(row, (requests, requests))
     column = jnp.sum(jnp.where(line == lane, rows, 0), axis=1, keepdims=True)
-    before = jnp.where((column == rows) & (line < lane), 1, 0)
-    rank = jnp.sum(before, axis=0, keepdims=True)
-    after = jnp.where((column == rows) & (lane < line), 1, 0)
-    rank_column = jnp.sum(after, axis=1, keepdims=True)
-    slot_ref[...] = jnp.where(row == group, rank, -1)
-    place_out_ref[...] = row * CAP + rank
-    mine = (column == group) & (rank_column == lane)
+    before = (column < rows) | ((column == rows) & (line < lane))
+    spot = jnp.sum(jnp.where(before, 1, 0), axis=0, keepdims=True)
+    before = (rows < column) | ((rows == column) & (lane < line))
+    spot_column = jnp.sum(jnp.where(before, 1, 0), axis=1, keepdims=True)
+    chips = CAP
+    slot_ref[...] = jnp.where(row == group, spot % chips, -1)
+    mine = (column == group) & (spot_column % chips == lane)
     index_ref[...] = jnp.sum(jnp.where(mine, line, 0), axis=0, keepdims=True)
+    device = 2 * (spot % chips) + spot // chips % 2
+    spot_ref[...] = device * (requests // (2 * chips)) + spot // (2 * chips)
+    core, chip = group % 2, group // 2
+    kept = spot_column == 2 * chips * lane + chips * core + chip
+    holder = jnp.sum(jnp.where(kept, column, 0), axis=0, keepdims=True)
+    source_ref[...] = jnp.where(holder % 2 == core, 0, chips) + holder // 2
 
 
 def pack(place, queries, tree, holder):
@@ -68,9 +74,10 @@
             line,
             line,
             line,
+            line,
         ),
         grid_spec=pltpu.PrefetchScalarGridSpec(
-            num_scalar_prefetch=1, grid=(), in_specs=[vmem] * 3, out_specs=(vmem,) * 4
+            num_scalar_prefetch=1, grid=(), in_specs=[vmem] * 3, out_specs=(vmem,) * 5
         ),
         compiler_params=pltpu.CompilerParams(vmem_limit_bytes=40 * 1024 * 1024),
         name="pack",
@@ -182,47 +189,62 @@
     )(slot, parents, picked, own, other)
 
 
-def project_kernel(place_ref, every_ref, weight_ref, out_ref, rows_ref, sems):
+def settle_kernel(source_ref, own_ref, other_ref, out_ref):
+    count, model = out_ref.shape[0], own_ref.shape[2]
+    chips = own_ref.shape[0]
+    for k in range(count):
+        source = source_ref[0, k]
+        chip = source % chips
+        rows = jnp.where(
+            source < chips, own_ref[chip].astype(jnp.float32), other_ref[chip].astype(jnp.float32)
+        )
+        power = exponent(rows)
+        out_ref[k, :, :model] = (rows * jnp.exp2(10.0 - power)).astype(jnp.bfloat16)
+        width = out_ref.shape[2] - model
+        out_ref[k, :, model:] = jnp.broadcast_to(power, (rows.shape[0], width)).astype(jnp.bfloat16)
+
+
+def settle(source, own, other, count):
+    nodes, model = own.shape[1:]
+    vmem = pl.BlockSpec(memory_space=pltpu.VMEM)
+    return pl.pallas_call(
+        settle_kernel,
+        out_shape=jax.ShapeDtypeStruct((count, nodes, model + 128), jnp.bfloat16),
+        grid_spec=pltpu.PrefetchScalarGridSpec(
+            num_scalar_prefetch=1, grid=(), in_specs=[vmem] * 2, out_specs=vmem
+        ),
+        compiler_params=pltpu.CompilerParams(vmem_limit_bytes=40 * 1024 * 1024),
+        name="settle",
+    )(source, own, other)
+
+
+def project_kernel(spot_ref, every_ref, weight_ref, out_ref):
     lanes, depth = out_ref.shape[0], weight_ref.shape[0]
-    requests, nodes = rows_ref.shape[0], rows_ref.shape[1]
-    share = requests // lanes
-    copies = []
-    for r in range(requests):
-        copy = pltpu.make_async_copy(every_ref.at[place_ref[0, r]], rows_ref.at[r], sems.at[r])
-        copy.start()
-        copies.append(copy)
+    share = every_ref.shape[0] // lanes
     for lane in range(lanes):
-        for copy in copies[lane * share : (lane + 1) * share]:
-            copy.wait()
-        block = rows_ref[lane * share : (lane + 1) * share].reshape(share * nodes, depth)
-        out_ref[lane] = jnp.dot(
-            block, weight_ref[...], preferred_element_type=jnp.float32
-        ).astype(jnp.bfloat16)
-
-
-def project(place, every, weight, lanes):
-    requests = place.shape[1]
-    nodes, depth = every.shape[1], every.shape[2]
+        block = jnp.concatenate(
+            [every_ref[spot_ref[0, lane * share + r]] for r in range(share)], axis=0
+        )
+        power = block[:, depth : depth + 1].astype(jnp.float32) - 10.0
+        product = jnp.dot(
+            block[:, :depth], weight_ref[...], preferred_element_type=jnp.float32
+        )
+        out_ref[lane] = (product * jnp.exp2(power)).astype(jnp.bfloat16)
+
+
+def project(spot, every, weight, lanes):
+    requests, nodes = every.shape[:2]
     columns = weight.shape[1]
+    vmem = pl.BlockSpec(memory_space=pltpu.VMEM)
     return pl.pallas_call(
         project_kernel,
         out_shape=jax.ShapeDtypeStruct((lanes, requests // lanes * nodes, columns), jnp.bfloat16),
         grid_spec=pltpu.PrefetchScalarGridSpec(
-            num_scalar_prefetch=1,
-            grid=(),
-            in_specs=[
-                pl.BlockSpec(memory_space=pl.ANY),
-                pl.BlockSpec(memory_space=pltpu.VMEM),
-            ],
-            out_specs=pl.BlockSpec(memory_space=pltpu.VMEM),
-            scratch_shapes=[
-                pltpu.VMEM((requests, nodes, depth), jnp.bfloat16),
-                pltpu.SemaphoreType.DMA((requests,)),
-            ],
+            num_scalar_prefetch=1, grid=(), in_specs=[vmem] * 2, out_specs=vmem
         ),
         compiler_params=pltpu.CompilerParams(vmem_limit_bytes=40 * 1024 * 1024),
         name="project",
-    )(place, every, weight)
+    )(spot, every, weight)
 
 
 def local(queries, tree_kv, prefix_kv, request_holder, parents, out_weight):
@@ -234,12 +256,16 @@
     own_half = prefix_kv[0, 0]
     other_half = swapped(own_half, "tensor", 0)
     here = jnp.stack([group, lane // 2]).astype(jnp.int32)
-    packed, slot, index, place = pack(here, queries, tree_kv, request_holder)
+    packed, slot, index, spot, source = pack(here, queries, tree_kv, request_holder)
     packed = lax.all_gather(packed.astype(jnp.float16), "dp", axis=0, tiled=True)
     picked = packed.at[index[0, :CAP]].get(mode="promise_in_bounds").astype(jnp.bfloat16)
     attended = attend(slot, parents, picked, own_half, other_half)
-    every = lax.all_gather(attended, "dp", axis=0, tiled=True)
-    partial = project(place, every, out_weight, lanes)
+    groups = lax.axis_size("dp")
+    along = [[i for i in range(groups) if i % 2 == core] for core in range(2)]
+    spread = lax.all_to_all(attended, "dp", 0, 0, axis_index_groups=along, tiled=True)
+    settled = settle(source, spread, swapped(spread, "dp", 0), requests // groups)
+    every = lax.all_gather(settled.astype(jnp.float16), "dp", axis=0, tiled=True)
+    partial = project(spot, every.astype(jnp.bfloat16), out_weight, lanes)
     shares = lax.all_to_all(partial, "tensor", 0, 0, tiled=True)
     total = jnp.sum(shares.astype(jnp.float32), axis=0).astype(jnp.bfloat16)
     return total.reshape(requests // lanes, nodes, out_weight.shape[1])

time: 244 us -> 204 us (0.84)
  waiting for transfers between devices: 103 us -> 1.52 us
  blocking collectives: 91.2 us -> 167 us
  between operations: 13.5 us -> 0.14 us
  Pallas kernels: 24.6 us -> 13.4 us
  starting transfers between devices: 4.16 us -> 12.8 us
    all_gather x1 -> x0, waiting for transfers between devices: 103 us -> none  [local(): every = lax.all_gather(attended, 'dp', axis=0, tiled=True)]
    all_gather x0 -> x1, blocking collectives: none -> 46.9 us  [local(): lax.all_gather(settled.astype(jnp.float16), 'dp', axis=0, tiled=True)]
    all_to_all x0 -> x1, blocking collectives: none -> 29.6 us  [local(): lax.all_to_all(attended, 'dp', 0, 0, axis_index_groups=along, tiled=True)]
    ppermute x1 -> x2, starting transfers between devices: 4.15 us -> 12.8 us  [swapped(): lax.ppermute(x, axis, [(i, i ^ 1 << bit) for i in range(lax.axis_size(axi...]
    pallas_call x1, Pallas kernels: 15.8 us -> 8.8 us  [attend(): pl.pallas_call(attend_kernel, out_shape=jax.ShapeDtypeStruct((CAP, nodes,...]
    pallas_call x1, Pallas kernels: 7.86 us -> 2.98 us  [project(): pl.pallas_call(project_kernel, out_shape=jax.ShapeDtypeStruct((lanes, req...]
where the time goes in v3:
time: 204 us
  blocking collectives  167 us (82%)
  Pallas kernels  13.4 us (7%)
  starting transfers between devices  12.8 us (6%)
  local copies, waits for them, and re-layouts  6.61 us (3%)
    all_gather x1, blocking collectives, local(): lax.all_gather(packed.astype(jnp.float16), 'dp', axis=0, tiled=True)  57.7 us
    all_gather x1, blocking collectives, local(): lax.all_gather(settled.astype(jnp.float16), 'dp', axis=0, tiled=True)  46.9 us
    all_to_all x1, blocking collectives, local(): shares = lax.all_to_all(partial, 'tensor', 0, 0, tiled=True)  33.3 us
    all_to_all x1, blocking collectives, local(): lax.all_to_all(attended, 'dp', 0, 0, axis_index_groups=along, tiled=True)  29.6 us
    ppermute x2, starting transfers between devices, swapped(): lax.ppermute(x, axis, [(i, i ^ 1 << bit) for i in range(lax.axis_size(axi...  12.8 us
    pallas_call x1, Pallas kernels, attend(): pl.pallas_call(attend_kernel, out_shape=jax.ShapeDtypeStruct((CAP, nodes,...  8.8 us
  transfers between devices with their start and end apart: 2, of which 1 were waited for; matrix products, arithmetic and copies ran while one was open for 2% of the time, Pallas kernels for 0%

profile of v3, /device:TPU:1, one launch (start us, length us, event | category | flops | bytes accessed | tf_op | source)
XLA Modules:
  0.0 203.8 jit_solution(18314828327431357521)
XLA Ops:
  0.0 0.0 copy-start.5
  0.0 4.2 %collective-permute-start = (bf16[1024,256]{1,0:T(8,128)(2,1)}, bf16[1024,256]{1,0:T(8,128)(2,1)S(1)}, u32[]{:S(2)}, u32[]{:S(2)}) collective-permute-start(bf16[1024,256]{1,0:T(8,128)(2,1)} %bitcast.9), channel_id=1, source_target_pairs={{0,1},{1,0},{2,3},{3,2},{4,5},{5,4},{6,7},{7,6},{8,9},{9,8},{10,11... | collective-permute-start | bytes 1572872 | tf_op jit(solution)/shard_map/ppermute | solution.py:17
  4.2 0.1 pad_add_fusion.place_ref
  4.3 0.0 copy-start.2
  4.3 0.9 copy-done.2
  5.2 0.0 copy-start.3
  5.2 0.9 copy-done.3
  6.1 0.0 copy-start.4
  6.1 0.7 copy-done.4
  6.8 0.9 pack.1
  7.7 0.0 copy-start.1
  7.7 57.7 %all-gather.2 = f16[128,16,1408]{2,1,0:T(8,128)(2,1)} all-gather(f16[4,16,1408]{2,1,0:T(8,128)(2,1)S(1)} %convert_element_type.14), channel_id=1, replica_groups=mesh['dp'=32,'tensor'=16] {'dp'}, dimensions={0}, use_global_device_ids=true | all-gather | bytes 5947392 | tf_op jit(solution)/shard_map/all_gather | solution.py:260
  65.4 0.0 copy-done.5
  65.4 0.1 copy.8.parents_ref
  65.6 3.5 %gather_fusion = f16[16,16,1408]{2,1,0:T(8,128)(2,1)S(1)} fusion(f16[128,16,1408]{2,1,0:T(8,128)(2,1)} %all-gather.2, s32[1024]{0:T(1024)S(1)} %pad_clamp_fusion), kind=kCustom, calls=%fused_computation | custom fusion | bytes 1441856 | tf_op jit(solution)/shard_map/gather | solution.py:261
  69.1 0.1 convert_element_type.15.picked_ref
  69.2 0.0 collective-permute-done.other_ref
  69.2 0.0 copy-done.1
  69.2 8.8 %attend.1 = bf16[16,16,1024]{2,1,0:T(8,128)(2,1)S(1)} custom-call(s32[1,128]{1,0:T(1,128)S(1)} %get-tuple-element.12.slot_ref, s32[128,16]{1,0:T(8,128)S(1)} %copy.8.parents_ref, bf16[16,16,1408]{2,1,0:T(8,128)(2,1)S(1)} %convert_element_type.15.picked_ref, bf16[1024,256]{1,0:T(8,128)(2,1)S(1)} %bitcast.10, bf16[1024,256]{1,0:T(8,128)(2,1)S(1)} %collective-permute-done.other_ref), custom_call_target="tpu_custom_call" | custom-call | tf_op jit(solution)/shard_map/attend/pallas_call | solution.py:171
  78.0 29.6 %all_to_all.10.own_ref = bf16[16,16,1024]{2,1,0:T(8,128)(2,1)S(1)} all-to-all(bf16[16,16,1024]{2,1,0:T(8,128)(2,1)S(1)} %attend.1), channel_id=1, replica_groups={{0,32,64,96,128,160,192,224,256,288,320,352,384,416,448,480},{16,48,80,..., dimensions={0} | all-to-all | bytes 1048576 | tf_op jit(solution)/shard_map/all_to_all | solution.py:265
  107.6 8.6 %collective-permute-start.1 = (bf16[16,16,1024]{2,1,0:T(8,128)(2,1)S(1)}, bf16[16,16,1024]{2,1,0:T(8,128)(2,1)S(1)}, u32[]{:S(2)}, u32[]{:S(2)}) collective-permute-start(bf16[16,16,1024]{2,1,0:T(8,128)(2,1)S(1)} %all_to_all.10.own_ref), channel_id=1, source_target_pairs={{0,16},{16,0},{32,48},{48,32},{64,80},{80,64},{96,112},{112,96},{1... | collective-permute-start | bytes 1572872 | tf_op jit(solution)/shard_map/ppermute | solution.py:17
  116.3 1.5 collective-permute-done.1.other_ref
  117.8 0.7 settle.1
  118.5 46.9 %all-gather.3 = f16[128,16,1152]{2,1,0:T(8,128)(2,1)S(1)} all-gather(f16[4,16,1152]{2,1,0:T(8,128)(2,1)S(1)} %convert_element_type.16), channel_id=1, replica_groups=mesh['dp'=32,'tensor'=16] {'dp'}, dimensions={0}, use_global_device_ids=true | all-gather | bytes 4866048 | tf_op jit(solution)/shard_map/all_gather | solution.py:267
  165.4 0.0 copy-start
  165.4 0.7 convert_element_type.17.every_ref
  166.1 0.5 copy-done
  166.6 3.0 %project.1 = bf16[16,128,512]{2,1,0:T(8,128)(2,1)S(1)} custom-call(s32[1,128]{1,0:T(1,128)S(1)} %get-tuple-element.10.spot_ref, bf16[128,16,1152]{2,1,0:T(8,128)(2,1)S(1)} %convert_element_type.17.every_ref, bf16[1024,512]{1,0:T(8,128)(2,1)S(1)} %copy-done), custom_call_target="tpu_custom_call" | custom-call | tf_op jit(solution)/shard_map/project/pallas_call | solution.py:239
  169.6 33.3 %all_to_all.11 = bf16[16,128,512]{2,1,0:T(8,128)(2,1)S(1)} all-to-all(bf16[16,128,512]{2,1,0:T(8,128)(2,1)S(1)} %project.1), channel_id=1, replica_groups=mesh['dp'=32,'tensor'=16] {'tensor'}, dimensions={0} | all-to-all | bytes 4194304 | tf_op jit(solution)/shard_map/all_to_all | solution.py:269
  202.9 1.0 reduce_sum.12
  (4 shorter events, 0.1 us)
Async XLA Ops:
  0.0 65.4 %copy-start.5 = (s32[128,16]{0,1:T(8,128)S(1)}, s32[128,16]{0,1:T(8,128)}, u32[]{:S(2)}) copy-start(s32[128,16]{0,1:T(8,128)} %param.10) | copy-start | bytes 24580
  0.0 69.2 %collective-permute-start = (bf16[1024,256]{1,0:T(8,128)(2,1)}, bf16[1024,256]{1,0:T(8,128)(2,1)S(1)}, u32[]{:S(2)}, u32[]{:S(2)}) collective-permute-start(bf16[1024,256]{1,0:T(8,128)(2,1)} %bitcast.9), channel_id=1, source_target_pairs={{0,1},{1,0},{2,3},{3,2},{4,5},{5,4},{6,7},{7,6},{8,9},{9,8},{10,11... | collective-permute-start | bytes 1572872 | tf_op jit(solution)/shard_map/ppermute | solution.py:17
  4.3 1.0 copy-start.2
  5.2 0.9 copy-start.3
  6.1 0.7 copy-start.4
  7.7 61.5 %copy-start.1 = (bf16[1,1,1024,256]{3,2,1,0:T(8,128)(2,1)S(1)}, bf16[1,1,1024,256]{3,2,1,0:T(8,128)(2,1)}, u32[]{:S(2)}) copy-start(bf16[1,1,1024,256]{3,2,1,0:T(8,128)(2,1)} %param.8) | copy-start | bytes 1572868
  107.6 10.2 %collective-permute-start.1 = (bf16[16,16,1024]{2,1,0:T(8,128)(2,1)S(1)}, bf16[16,16,1024]{2,1,0:T(8,128)(2,1)S(1)}, u32[]{:S(2)}, u32[]{:S(2)}) collective-permute-start(bf16[16,16,1024]{2,1,0:T(8,128)(2,1)S(1)} %all_to_all.10.own_ref), channel_id=1, source_target_pairs={{0,16},{16,0},{32,48},{48,32},{64,80},{80,64},{96,112},{112,96},{1... | collective-permute-start | bytes 1572872 | tf_op jit(solution)/shard_map/ppermute | solution.py:17
  165.4 1.2 copy-start

commit v4 on v3

--- a/solution.py
+++ b/solution.py
@@ -10,35 +10,62 @@
 CAP = 16
 PAIR = 8
 NEG = -1e30
-RAISE = 2.0**11
+LIFT = 2.0**59
 
 
 def swapped(x, axis, bit):
     return lax.ppermute(x, axis, [(i, i ^ 1 << bit) for i in range(lax.axis_size(axis))])
 
 
-def exponent(x):
-    peak = jnp.max(jnp.abs(x), axis=-1, keepdims=True)
-    return jnp.floor(jnp.log2(jnp.clip(peak, 2.0**-100, 2.0**6)))
-
-
-def pack_kernel(place_ref, queries_ref, tree_ref, holder_ref, packed_ref, slot_ref, index_ref, spot_ref, source_ref):
+def encode(x):
+    root = jnp.sqrt(jnp.sqrt(jnp.abs(x) * LIFT))
+    return jnp.where(x < 0, -root, root)
+
+
+def decode(x):
+    x = x.astype(jnp.float32)
+    return ((x * jnp.abs(x)) * ((x * (1.0 / LIFT)) * x)).astype(jnp.bfloat16)
+
+
+def pack_kernel(
+    place_ref,
+    queries_hbm,
+    tree_hbm,
+    holder_hbm,
+    packed_ref,
+    slot_ref,
+    index_ref,
+    spot_ref,
+    source_ref,
+    queries_ref,
+    tree_ref,
+    holder_ref,
+    sems,
+):
     group, column = place_ref[0], place_ref[1]
     count, nodes, model = queries_ref.shape
     kv_heads, width = tree_ref.shape[2], tree_ref.shape[3] // 2
+    copies = [
+        pltpu.make_async_copy(source, target, sems.at[k])
+        for k, (source, target) in enumerate(
+            ((holder_hbm, holder_ref), (queries_hbm, queries_ref), (tree_hbm, tree_ref))
+        )
+    ]
+    for copy in copies:
+        copy.start()
+    copies[0].wait()
+    plan(group, holder_ref, slot_ref, index_ref, spot_ref, source_ref)
+    copies[1].wait()
+    for r in range(count):
+        packed_ref[r, :, :model] = encode(queries_ref[r].astype(jnp.float32))
+    copies[2].wait()
     pick = lax.broadcasted_iota(jnp.int32, (nodes, kv_heads, 2 * width), 1) == column
     for r in range(count):
-        packed_ref[r, :, :model] = (queries_ref[r].astype(jnp.float32) * RAISE).astype(jnp.bfloat16)
         tree = jnp.sum(jnp.where(pick, tree_ref[r].astype(jnp.float32), 0.0), axis=1)
-        packed_ref[r, :, model : model + width] = (tree[:, :width] * RAISE).astype(jnp.bfloat16)
-        values = tree[:, width:]
-        power = exponent(values)
-        packed_ref[r, :, model + width : model + 2 * width] = (
-            values * jnp.exp2(10.0 - power)
-        ).astype(jnp.bfloat16)
-        packed_ref[r, :, model + 2 * width :] = jnp.broadcast_to(power, values.shape).astype(
-            jnp.bfloat16
-        )
+        packed_ref[r, :, model:] = encode(tree)
+
+
+def plan(group, holder_ref, slot_ref, index_ref, spot_ref, source_ref):
     requests = holder_ref.shape[1]
     line = lax.broadcasted_iota(jnp.int32, (requests, requests), 0)
     lane = lax.broadcasted_iota(jnp.int32, (requests, requests), 1)
@@ -66,29 +93,40 @@
     width = tree.shape[3] // 2
     requests = holder.shape[0]
     vmem = pl.BlockSpec(memory_space=pltpu.VMEM)
+    hbm = pl.BlockSpec(memory_space=pltpu.HBM)
     line = jax.ShapeDtypeStruct((1, requests), jnp.int32)
+    holder = holder.reshape(1, requests)
     return pl.pallas_call(
         pack_kernel,
         out_shape=(
-            jax.ShapeDtypeStruct((count, nodes, model + 3 * width), jnp.bfloat16),
+            jax.ShapeDtypeStruct((count, nodes, model + 2 * width), jnp.float32),
             line,
             line,
             line,
             line,
         ),
         grid_spec=pltpu.PrefetchScalarGridSpec(
-            num_scalar_prefetch=1, grid=(), in_specs=[vmem] * 3, out_specs=(vmem,) * 5
-        ),
-        compiler_params=pltpu.CompilerParams(vmem_limit_bytes=40 * 1024 * 1024),
+            num_scalar_prefetch=1,
+            grid=(),
+            in_specs=[hbm] * 3,
+            out_specs=(vmem,) * 5,
+            scratch_shapes=[
+                pltpu.VMEM(queries.shape, queries.dtype),
+                pltpu.VMEM(tree.shape, tree.dtype),
+                pltpu.VMEM(holder.shape, holder.dtype),
+                pltpu.SemaphoreType.DMA((3,)),
+            ],
+        ),
+        compiler_params=pltpu.CompilerParams(vmem_limit_bytes=60 * 1024 * 1024),
         name="pack",
-    )(place, queries, tree, holder.reshape(1, requests))
-
-
-def attend_kernel(slot_ref, parents_ref, picked_ref, own_ref, other_ref, out_ref, reach_ref, value_ref):
+    )(place, queries, tree, holder)
+
+
+def attend_kernel(index_ref, slot_ref, parents_ref, packed_ref, own_ref, other_ref, out_ref, reach_ref, value_ref):
     step = pl.program_id(0)
-    nodes = picked_ref.shape[1]
+    nodes = packed_ref.shape[1]
     width = own_ref.shape[1] // 2
-    heads = (picked_ref.shape[2] - 3 * width) // width
+    heads = (packed_ref.shape[2] - 2 * width) // width
     half = own_ref.shape[0]
     rows = CAP * nodes
 
@@ -117,12 +155,13 @@
         value_ref[pl.ds(half, half), :width] = other_ref[:, width:]
         value_ref[:, width:] = jnp.ones((2 * half, width), jnp.bfloat16)
 
-    scale = 1.0 / math.sqrt(width) * math.log2(math.e) / RAISE
+    scale = 1.0 / math.sqrt(width) * math.log2(math.e)
+    places = [index_ref[0, step * PAIR + s] for s in range(PAIR)]
     query = jnp.concatenate(
-        [picked_ref[s, :, h * width : (h + 1) * width] for s in range(PAIR) for h in range(heads)],
+        [packed_ref[r, :, h * width : (h + 1) * width] for r in places for h in range(heads)],
         axis=0,
     )
-    tree = jnp.concatenate([picked_ref[s, :, heads * width :] for s in range(PAIR)], axis=0)
+    tree = jnp.concatenate([packed_ref[r, :, heads * width :] for r in places], axis=0)
     dims = (((1,), (1,)), ((), ()))
     span = PAIR * nodes
     mask = jnp.zeros((span, span), jnp.float32)
@@ -133,14 +172,10 @@
         [mask[s * nodes : (s + 1) * nodes] for s in range(PAIR) for h in range(heads)], axis=0
     )
     drafts = lax.dot_general(query, tree[:, :width], dims, preferred_element_type=jnp.float32)
-    drafts = jnp.where(mask > 0, drafts * (1.0 / RAISE), NEG)
+    drafts = jnp.where(mask > 0, drafts, NEG)
     peak = jnp.max(drafts, axis=1, keepdims=True)
     drafts = (jnp.exp2((drafts - peak) * scale) * mask).astype(jnp.bfloat16)
-    power = tree[:, 2 * width :].astype(jnp.float32) - 10.0
-    tree_value = (tree[:, width : 2 * width].astype(jnp.float32) * jnp.exp2(power)).astype(
-        jnp.bfloat16
-    )
-    tree_value = jnp.concatenate([tree_value, jnp.ones((span, width), jnp.bfloat16)], axis=1)
+    tree_value = jnp.concatenate([tree[:, width:], jnp.ones((span, width), jnp.bfloat16)], axis=1)
     peaks = [peak]
     sums = [jnp.dot(drafts, tree_value, preferred_element_type=jnp.float32)]
     for k, ref in enumerate((own_ref, other_ref)):
@@ -162,46 +197,41 @@
             out_ref[s, :, h * width : (h + 1) * width] = attended[start : start + nodes]
 
 
-def attend(slot, parents, picked, own, other):
-    nodes = picked.shape[1]
-    depth = picked.shape[2]
+def attend(index, slot, parents, packed, own, other):
+    nodes, depth = packed.shape[1:]
     width = own.shape[1] // 2
     half = own.shape[0]
-    model = depth - 3 * width
+    model = depth - 2 * width
     return pl.pallas_call(
         attend_kernel,
         out_shape=jax.ShapeDtypeStruct((CAP, nodes, model), jnp.bfloat16),
-        grid=(CAP // PAIR,),
-        in_specs=[
-            pl.BlockSpec(slot.shape, lambda i: (0, 0)),
-            pl.BlockSpec(parents.shape, lambda i: (0, 0)),
-            pl.BlockSpec((PAIR, nodes, depth), lambda i: (i, 0, 0)),
-            pl.BlockSpec((half, 2 * width), lambda i: (0, 0)),
-            pl.BlockSpec((half, 2 * width), lambda i: (0, 0)),
-        ],
-        out_specs=pl.BlockSpec((PAIR, nodes, model), lambda i: (i, 0, 0)),
-        scratch_shapes=[
-            pltpu.VMEM((CAP * nodes, CAP * nodes), jnp.float32),
-            pltpu.VMEM((2 * half, 2 * width), jnp.bfloat16),
-        ],
-        compiler_params=pltpu.CompilerParams(vmem_limit_bytes=40 * 1024 * 1024),
+        grid_spec=pltpu.PrefetchScalarGridSpec(
+            num_scalar_prefetch=1,
+            grid=(CAP // PAIR,),
+            in_specs=[pl.BlockSpec(memory_space=pltpu.VMEM)] * 5,
+            out_specs=pl.BlockSpec((PAIR, nodes, model), lambda i, index: (i, 0, 0)),
+            scratch_shapes=[
+                pltpu.VMEM((CAP * nodes, CAP * nodes), jnp.float32),
+                pltpu.VMEM((2 * half, 2 * width), jnp.bfloat16),
+            ],
+        ),
+        compiler_params=pltpu.CompilerParams(vmem_limit_bytes=28 * 1024 * 1024),
         name="attend",
-    )(slot, parents, picked, own, other)
+    )(index, slot, parents, packed, own, other)
 
 
 def settle_kernel(source_ref, own_ref, other_ref, out_ref):
-    count, model = out_ref.shape[0], own_ref.shape[2]
     chips = own_ref.shape[0]
-    for k in range(count):
+    for k in range(out_ref.shape[0]):
         source = source_ref[0, k]
         chip = source % chips
-        rows = jnp.where(
-            source < chips, own_ref[chip].astype(jnp.float32), other_ref[chip].astype(jnp.float32)
-        )
-        power = exponent(rows)
-        out_ref[k, :, :model] = (rows * jnp.exp2(10.0 - power)).astype(jnp.bfloat16)
-        width = out_ref.shape[2] - model
-        out_ref[k, :, model:] = jnp.broadcast_to(power, (rows.shape[0], width)).astype(jnp.bfloat16)
+        out_ref[k] = encode(
+            jnp.where(
+                source < chips,
+                own_ref[chip].astype(jnp.float32),
+                other_ref[chip].astype(jnp.float32),
+            )
+        )
 
 
 def settle(source, own, other, count):
@@ -209,7 +239,7 @@
     vmem = pl.BlockSpec(memory_space=pltpu.VMEM)
     return pl.pallas_call(
         settle_kernel,
-        out_shape=jax.ShapeDtypeStruct((count, nodes, model + 128), jnp.bfloat16),
+        out_shape=jax.ShapeDtypeStruct((count, nodes, model), jnp.float32),
         grid_spec=pltpu.PrefetchScalarGridSpec(
             num_scalar_prefetch=1, grid=(), in_specs=[vmem] * 2, out_specs=vmem
         ),
@@ -219,17 +249,15 @@
 
 
 def project_kernel(spot_ref, every_ref, weight_ref, out_ref):
-    lanes, depth = out_ref.shape[0], weight_ref.shape[0]
+    lanes = out_ref.shape[0]
     share = every_ref.shape[0] // lanes
     for lane in range(lanes):
         block = jnp.concatenate(
             [every_ref[spot_ref[0, lane * share + r]] for r in range(share)], axis=0
         )
-        power = block[:, depth : depth + 1].astype(jnp.float32) - 10.0
-        product = jnp.dot(
-            block[:, :depth], weight_ref[...], preferred_element_type=jnp.float32
-        )
-        out_ref[lane] = (product * jnp.exp2(power)).astype(jnp.bfloat16)
+        out_ref[lane] = jnp.dot(
+            block, weight_ref[...], preferred_element_type=jnp.float32
+        ).astype(jnp.bfloat16)
 
 
 def project(spot, every, weight, lanes):
@@ -258,14 +286,15 @@
     here = jnp.stack([group, lane // 2]).astype(jnp.int32)
     packed, slot, index, spot, source = pack(here, queries, tree_kv, request_holder)
     packed = lax.all_gather(packed.astype(jnp.float16), "dp", axis=0, tiled=True)
-    picked = packed.at[index[0, :CAP]].get(mode="promise_in_bounds").astype(jnp.bfloat16)
-    attended = attend(slot, parents, picked, own_half, other_half)
+    packed = decode(packed)
+    attended = attend(index, slot, parents, packed, own_half, other_half)
     groups = lax.axis_size("dp")
     along = [[i for i in range(groups) if i % 2 == core] for core in range(2)]
     spread = lax.all_to_all(attended, "dp", 0, 0, axis_index_groups=along, tiled=True)
     settled = settle(source, spread, swapped(spread, "dp", 0), requests // groups)
     every = lax.all_gather(settled.astype(jnp.float16), "dp", axis=0, tiled=True)
-    partial = project(spot, every.astype(jnp.bfloat16), out_weight, lanes)
+    every = decode(every)
+    partial = project(spot, every, out_weight, lanes)
     shares = lax.all_to_all(partial, "tensor", 0, 0, tiled=True)
     total = jnp.sum(shares.astype(jnp.float32), axis=0).astype(jnp.bfloat16)
     return total.reshape(requests // lanes, nodes, out_weight.shape[1])

time: 204 us -> 206 us (level)
  other arithmetic: 1.92 us -> 9.14 us
  local copies, waits for them, and re-layouts: 6.61 us -> 2.6 us
  blocking collectives: 167 us -> 163 us
  Pallas kernels: 13.4 us -> 16.1 us
    convert_element_type x2, other arithmetic: 0.81 us -> 6.5 us  [decode(): return (x * jnp.abs(x) * (x * (1.0 / LIFT) * x)).astype(jnp.bfloat16)]
    gather x1 -> x0, local copies, waits for them, and re-layouts: 3.5 us -> none  [local(): packed.at[index[0, :CAP]].get(mode='promise_in_bounds').astype(jnp.bfloat16)]
    all_gather x1, blocking collectives: 57.7 us -> 54.9 us  [local(): lax.all_gather(packed.astype(jnp.float16), 'dp', axis=0, tiled=True)]
    pallas_call x1, Pallas kernels: 0.89 us -> 3 us  [pack(): pl.pallas_call(pack_kernel, out_shape=(jax.ShapeDtypeStruct((count, nodes...]
  transfers between devices with their start and end apart: 2 -> 2, of which waited for: 1 -> 1; matrix products, arithmetic and copies ran while one was open for 2% -> 3% of each run, Pallas kernels for 0% -> 1%
where the time goes in v4:
time: 206 us; the launch traced here: 205 us
  blocking collectives  163 us (79%)
  Pallas kernels  16.1 us (8%)
  starting transfers between devices  12.7 us (6%)
  other arithmetic  9.14 us (4%)
  local copies, waits for them, and re-layouts  2.6 us (1%)
    all_gather x1, blocking collectives, local(): lax.all_gather(packed.astype(jnp.float16), 'dp', axis=0, tiled=True)  54.9 us
    all_gather x1, blocking collectives, local(): lax.all_gather(settled.astype(jnp.float16), 'dp', axis=0, tiled=True)  45.5 us
    all_to_all x1, blocking collectives, local(): shares = lax.all_to_all(partial, 'tensor', 0, 0, tiled=True)  33.3 us
    all_to_all x1, blocking collectives, local(): lax.all_to_all(attended, 'dp', 0, 0, axis_index_groups=along, tiled=True)  29.7 us
    ppermute x2, starting transfers between devices, swapped(): lax.ppermute(x, axis, [(i, i ^ 1 << bit) for i in range(lax.axis_size(axi...  12.7 us
    pallas_call x1, Pallas kernels, attend(): pl.pallas_call(attend_kernel, out_shape=jax.ShapeDtypeStruct((CAP, nodes,...  9.44 us
    convert_element_type x2, other arithmetic, decode(): return (x * jnp.abs(x) * (x * (1.0 / LIFT) * x)).astype(jnp.bfloat16)  6.5 us
  transfers between devices with their start and end apart: 2, of which 1 were waited for; matrix products, arithmetic and copies ran while one was open for 3% of the time, Pallas kernels for 1%

profile of v4, /device:TPU:1, one launch (start us, length us, event | category | flops | bytes accessed | tf_op | source)
XLA Modules:
  0.0 205.5 jit_solution(5609149948380631187)
XLA Ops:
  0.0 4.0 %collective-permute-start = (bf16[1024,256]{1,0:T(8,128)(2,1)}, bf16[1024,256]{1,0:T(8,128)(2,1)S(1)}, u32[]{:S(2)}, u32[]{:S(2)}) collective-permute-start(bf16[1024,256]{1,0:T(8,128)(2,1)} %bitcast.5), channel_id=1, source_target_pairs={{0,1},{1,0},{2,3},{3,2},{4,5},{5,4},{6,7},{7,6},{8,9},{9,8},{10,11... | collective-permute-start | bytes 1572872 | tf_op jit(solution)/shard_map/ppermute | solution.py:17
  4.0 0.7 pad_add_fusion.place_ref
  4.7 3.0 %pack.1 = (f32[4,16,1280]{2,1,0:T(8,128)}, s32[1,128]{1,0:T(1,128)}, s32[1,128]{1,0:T(1,128)}, s32[1,128]{1,0:T(1,128)}, s32[1,128]{1,0:T(1,128)}) custom-call(s32[2]{0:T(128)} %pad_add_fusion.place_ref, bf16[4,16,1024]{2,1,0:T(8,128)(2,1)} %queries_hbm.1, bf16[4,16,8,256]{3,2,1,0:T(8,128)(2,1)} %tree_hbm.1, s32[1,128]{1,0:T(1,128)} %bitcast.7), custom_call_target="tpu_custom_call" | custom-call | tf_op jit(solution)/shard_map/pack/pallas_call | solution.py:99
  7.7 1.0 convert_element_type.20
  8.7 54.9 %all-gather.2 = f16[128,16,1280]{2,1,0:T(8,128)(2,1)S(1)} all-gather(f16[4,16,1280]{2,1,0:T(8,128)(2,1)S(1)} %convert_element_type.20), channel_id=1, replica_groups=mesh['dp'=32,'tensor'=16] {'dp'}, dimensions={0}, use_global_device_ids=true | all-gather | bytes 5406720 | tf_op jit(solution)/shard_map/all_gather | solution.py:288
  63.6 0.0 copy-start.7
  63.6 0.0 copy-start.2
  63.6 0.0 copy-start.4
  63.6 0.0 copy-start.5
  63.6 4.6 %fusion.1.packed_ref = bf16[128,16,1280]{2,1,0:T(8,128)(2,1)} fusion(f16[128,16,1280]{2,1,0:T(8,128)(2,1)S(1)} %all-gather.2), kind=kLoop, calls=%fused_computation.9 | loop fusion | flops 18350080 | bytes 10485760 | tf_op jit(solution)/shard_map/convert_element_type | solution.py:27
  68.2 0.0 copy-done.7
  68.2 0.0 copy-start.3
  68.2 0.1 copy.8.parents_ref
  68.3 0.0 collective-permute-done.other_ref
  68.3 0.0 copy-done.2
  68.3 0.0 copy-done.4
  68.3 0.0 copy-done.5
  68.3 0.0 copy-start
  68.3 2.5 %copy-done = bf16[128,16,1280]{2,1,0:T(8,128)(2,1)S(1)} copy-done((bf16[128,16,1280]{2,1,0:T(8,128)(2,1)S(1)}, bf16[128,16,1280]{2,1,0:T(8,128)(2,1)}, u32[]{:S(2)}) %copy-start) | copy-done | bytes 5242904
  70.8 9.4 %attend.1 = bf16[16,16,1024]{2,1,0:T(8,128)(2,1)S(1)} custom-call(s32[1,128]{1,0:T(1,128)S(1)} %copy-done.5, s32[1,128]{1,0:T(1,128)S(1)} %copy-done.4, s32[128,16]{1,0:T(8,128)S(1)} %copy.8.parents_ref, bf16[128,16,1280]{2,1,0:T(8,128)(2,1)S(1)} %copy-done, bf16[1024,256]{1,0:T(8,128)(2,1)S(1)} %bitcast.6, bf16[1024,256]{1,0:T(8,128)(2,1)S(1)} %collective-permute-done.other_ref), custom_call_target="tpu_custom_call" | custom-call | tf_op jit(solution)/shard_map/attend/pallas_call | solution.py:205
  80.2 29.7 %all_to_all.10.own_ref = bf16[16,16,1024]{2,1,0:T(8,128)(2,1)S(1)} all-to-all(bf16[16,16,1024]{2,1,0:T(8,128)(2,1)S(1)} %attend.1), channel_id=1, replica_groups={{0,32,64,96,128,160,192,224,256,288,320,352,384,416,448,480},{16,48,80,..., dimensions={0} | all-to-all | bytes 1048576 | tf_op jit(solution)/shard_map/all_to_all | solution.py:293
  109.9 8.7 %collective-permute-start.1 = (bf16[16,16,1024]{2,1,0:T(8,128)(2,1)S(1)}, bf16[16,16,1024]{2,1,0:T(8,128)(2,1)S(1)}, u32[]{:S(2)}, u32[]{:S(2)}) collective-permute-start(bf16[16,16,1024]{2,1,0:T(8,128)(2,1)S(1)} %all_to_all.10.own_ref), channel_id=1, source_target_pairs={{0,16},{16,0},{32,48},{48,32},{64,80},{80,64},{96,112},{112,96},{1... | collective-permute-start | bytes 1572872 | tf_op jit(solution)/shard_map/ppermute | solution.py:17
  118.6 1.5 collective-permute-done.1.other_ref
  120.1 0.0 copy-done.3
  120.1 0.7 settle.1
  120.9 45.5 %all-gather.3 = f16[128,16,1024]{2,1,0:T(8,128)(2,1)S(1)} all-gather(f16[4,16,1024]{2,1,0:T(8,128)(2,1)S(1)} %convert_element_type.23), channel_id=1, replica_groups=mesh['dp'=32,'tensor'=16] {'dp'}, dimensions={0}, use_global_device_ids=true | all-gather | bytes 4325376 | tf_op jit(solution)/shard_map/all_gather | solution.py:295
  166.4 0.0 copy-start.1
  166.4 0.0 copy-start.6
  166.4 1.9 fusion.3.every_ref
  168.3 0.0 copy-done.1
  168.3 0.0 copy-done.6
  168.3 2.9 %project.1 = bf16[16,128,512]{2,1,0:T(8,128)(2,1)S(1)} custom-call(s32[1,128]{1,0:T(1,128)S(1)} %copy-done.6, bf16[128,16,1024]{2,1,0:T(8,128)(2,1)S(1)} %fusion.3.every_ref, bf16[1024,512]{1,0:T(8,128)(2,1)S(1)} %copy-done.1), custom_call_target="tpu_custom_call" | custom-call | tf_op jit(solution)/shard_map/project/pallas_call | solution.py:267
  171.2 33.3 %all_to_all.11 = bf16[16,128,512]{2,1,0:T(8,128)(2,1)S(1)} all-to-all(bf16[16,128,512]{2,1,0:T(8,128)(2,1)S(1)} %project.1), channel_id=1, replica_groups=mesh['dp'=32,'tensor'=16] {'tensor'}, dimensions={0} | all-to-all | bytes 4194304 | tf_op jit(solution)/shard_map/all_to_all | solution.py:298
  204.5 1.0 reduce_sum.12
  (1 shorter events, 0.0 us)
Async XLA Ops:
  0.0 68.3 %collective-permute-start = (bf16[1024,256]{1,0:T(8,128)(2,1)}, bf16[1024,256]{1,0:T(8,128)(2,1)S(1)}, u32[]{:S(2)}, u32[]{:S(2)}) collective-permute-start(bf16[1024,256]{1,0:T(8,128)(2,1)} %bitcast.5), channel_id=1, source_target_pairs={{0,1},{1,0},{2,3},{3,2},{4,5},{5,4},{6,7},{7,6},{8,9},{9,8},{10,11... | collective-permute-start | bytes 1572872 | tf_op jit(solution)/shard_map/ppermute | solution.py:17
  63.6 4.6 %copy-start.7 = (s32[128,16]{0,1:T(8,128)S(1)}, s32[128,16]{0,1:T(8,128)}, u32[]{:S(2)}) copy-start(s32[128,16]{0,1:T(8,128)} %param.10) | copy-start | bytes 24580
  63.6 4.7 %copy-start.2 = (bf16[1,1,1024,256]{3,2,1,0:T(8,128)(2,1)S(1)}, bf16[1,1,1024,256]{3,2,1,0:T(8,128)(2,1)}, u32[]{:S(2)}) copy-start(bf16[1,1,1024,256]{3,2,1,0:T(8,128)(2,1)} %param.8) | copy-start | bytes 1572868
  63.6 4.7 %copy-start.4 = (s32[1,128]{1,0:T(1,128)S(1)}, s32[1,128]{1,0:T(1,128)}, u32[]{:S(2)}) copy-start(s32[1,128]{1,0:T(1,128)} %get-tuple-element.13.slot_ref) | copy-start | bytes 1540
  63.6 4.7 %copy-start.5 = (s32[1,128]{1,0:T(1,128)S(1)}, s32[1,128]{1,0:T(1,128)}, u32[]{:S(2)}) copy-start(s32[1,128]{1,0:T(1,128)} %get-tuple-element.12.index_ref) | copy-start | bytes 1540
  68.2 51.9 %copy-start.3 = (s32[1,128]{1,0:T(1,128)S(1)}, s32[1,128]{1,0:T(1,128)}, u32[]{:S(2)}) copy-start(s32[1,128]{1,0:T(1,128)} %get-tuple-element.11.source_ref) | copy-start | bytes 1540
  68.3 2.5 %copy-start = (bf16[128,16,1280]{2,1,0:T(8,128)(2,1)S(1)}, bf16[128,16,1280]{2,1,0:T(8,128)(2,1)}, u32[]{:S(2)}) copy-start(bf16[128,16,1280]{2,1,0:T(8,128)(2,1)} %fusion.1.packed_ref) | copy-start | bytes 15728644
  109.9 10.2 %collective-permute-start.1 = (bf16[16,16,1024]{2,1,0:T(8,128)(2,1)S(1)}, bf16[16,16,1024]{2,1,0:T(8,128)(2,1)S(1)}, u32[]{:S(2)}, u32[]{:S(2)}) collective-permute-start(bf16[16,16,1024]{2,1,0:T(8,128)(2,1)S(1)} %all_to_all.10.own_ref), channel_id=1, source_target_pairs={{0,16},{16,0},{32,48},{48,32},{64,80},{80,64},{96,112},{112,96},{1... | collective-permute-start | bytes 1572872 | tf_op jit(solution)/shard_map/ppermute | solution.py:17
  166.4 1.9 copy-start.1
  166.4 1.9 copy-start.6

commit v5 on v2

v5 whole, which is shorter than its diff:
```python
import functools
import math

import jax
import jax.numpy as jnp
from jax import lax
from jax.experimental import pallas as pl
from jax.experimental.pallas import tpu as pltpu
from jax.sharding import PartitionSpec as P

CAP = 16
PAIR = 16
BLOCK = 8
ROWS = (6, 7, 8, 16)
NEG = -1e30
LIFT = 2.0**59


def swapped(x, axis, bit):
    return lax.ppermute(x, axis, [(i, i ^ 1 << bit) for i in range(lax.axis_size(axis))])


def encode(x):
    root = jnp.sqrt(jnp.sqrt(jnp.abs(x) * LIFT))
    return jnp.where(x < 0, -root, root)


def decode(x):
    x = x.astype(jnp.float32)
    return ((x * jnp.abs(x)) * ((x * (1.0 / LIFT)) * x)).astype(jnp.bfloat16)


def pack_kernel(
    queries_ref, tree_ref, holder_ref, packed_ref, slot_ref, index_ref, spot_ref, source_ref, most_ref
):
    group, column = lax.axis_index("dp"), lax.axis_index("tensor") // 2
    count, nodes, model = queries_ref.shape
    kv_heads, width = tree_ref.shape[2], tree_ref.shape[3] // 2
    pick = lax.broadcasted_iota(jnp.int32, (nodes, kv_heads, 2 * width), 1) == column
    for r in range(count):
        packed_ref[r, :, :model] = encode(queries_ref[r].astype(jnp.float32))
        tree = jnp.sum(jnp.where(pick, tree_ref[r].astype(jnp.float32), 0.0), axis=1)
        packed_ref[r, :, model:] = encode(tree)
    requests = holder_ref.shape[1]
    line = lax.broadcasted_iota(jnp.int32, (requests, requests), 0)
    lane = lax.broadcasted_iota(jnp.int32, (requests, requests), 1)
    row = holder_ref[...]
    rows = jnp.broadcast_to(row, (requests, requests))
    column = jnp.sum(jnp.where(line == lane, rows, 0), axis=1, keepdims=True)

    def counted(chosen, axis):
        return jnp.sum(jnp.where(chosen, 1, 0), axis=axis, keepdims=True)

    same, earlier, later = column == rows, line < lane, lane < line
    block = (column >> 3) == (rows >> 3)
    rank, rank_line = counted(same & earlier, 0), counted(same & later, 1)
    place = counted(block & ((column < rows) | (same & earlier)), 0)
    place_line = counted(block & ((rows < column) | (same & later)), 1)
    slot = (place & 7) * 2 + (rank >> 3)
    slot_line = (place_line & 7) * 2 + (rank_line >> 3)
    slot_ref[...] = jnp.where(row == group, slot, -1)
    mine = (column == group) & (slot_line == lane)
    index_ref[...] = jnp.sum(jnp.where(mine, line, 0), axis=0, keepdims=True)
    device = (row >> 3) * BLOCK + (place & 7)
    for k, height in enumerate(ROWS):
        spot_ref[k : k + 1, :] = device * height + (place >> 3)
    kept = ((column >> 3) == (group >> 3)) & (place_line == BLOCK * lane + (group & 7))
    source = (column & 7) * 2 + (rank_line >> 3)
    source_ref[...] = jnp.sum(jnp.where(kept, source, 0), axis=0, keepdims=True)
    most = jnp.max(place, axis=1, keepdims=True) // BLOCK + 1
    choice = sum(jnp.where(most > height, 1, 0) for height in ROWS[:-1])
    most_ref[...] = jnp.broadcast_to(choice, most_ref.shape)


def pack(queries, tree, holder):
    count, nodes, model = queries.shape
    width = tree.shape[3] // 2
    requests = holder.shape[0]
    vmem = pl.BlockSpec(memory_space=pltpu.VMEM)
    line = jax.ShapeDtypeStruct((1, requests), jnp.int32)
    return pl.pallas_call(
        pack_kernel,
        out_shape=(
            jax.ShapeDtypeStruct((count, nodes, model + 2 * width), jnp.float32),
            line,
            line,
            jax.ShapeDtypeStruct((len(ROWS), requests), jnp.int32),
            line,
            line,
        ),
        in_specs=[vmem] * 3,
        out_specs=(vmem,) * 6,
        compiler_params=pltpu.CompilerParams(vmem_limit_bytes=40 * 1024 * 1024),
        name="pack",
    )(queries, tree, holder.reshape(1, requests))


def attend_kernel(slot_ref, parents_ref, picked_ref, own_ref, other_ref, out_ref, reach_ref, value_ref):
    step = pl.program_id(0)
    nodes = picked_ref.shape[1]
    width = own_ref.shape[1] // 2
    heads = (picked_ref.shape[2] - 2 * width) // width
    half = own_ref.shape[0]
    rows = CAP * nodes

    @pl.when(step == 0)
    def _():
        line = lax.broadcasted_iota(jnp.int32, (rows, rows), 0)
        column = lax.broadcasted_iota(jnp.int32, (rows, rows), 1)
        requests = slot_ref.shape[1]
        taken = lax.broadcasted_iota(jnp.int32, (rows, requests), 0) // nodes == slot_ref[...]
        above = jnp.dot(
            jnp.where(taken, 1.0, 0.0).astype(jnp.bfloat16),
            parents_ref[...].astype(jnp.float32).astype(jnp.bfloat16),
            preferred_element_type=jnp.float32,
        )
        node = lax.broadcasted_iota(jnp.int32, (rows, nodes), 0) % nodes
        own_node = lax.broadcasted_iota(jnp.int32, (rows, nodes), 1) == node
        above = jnp.sum(jnp.where(own_node, above, 0.0), axis=1, keepdims=True).astype(jnp.int32)
        above = (line // nodes) * nodes + above
        reach = jnp.where((column == line) | (column == above), 1.0, 0.0).astype(jnp.bfloat16)
        for level in range(4):
            reach = jnp.minimum(
                jnp.dot(reach, reach, preferred_element_type=jnp.float32), 1.0
            ).astype(jnp.bfloat16)
        reach_ref[...] = reach.astype(jnp.float32)
        value_ref[pl.ds(0, half), :width] = own_ref[:, width:]
        value_ref[pl.ds(half, half), :width] = other_ref[:, width:]
        value_ref[:, width:] = jnp.ones((2 * half, width), jnp.bfloat16)

    scale = 1.0 / math.sqrt(width) * math.log2(math.e)
    query = jnp.concatenate(
        [picked_ref[s, :, h * width : (h + 1) * width] for s in range(PAIR) for h in range(heads)],
        axis=0,
    )
    tree = jnp.concatenate([picked_ref[s, :, heads * width :] for s in range(PAIR)], axis=0)
    dims = (((1,), (1,)), ((), ()))
    span = PAIR * nodes
    mask = jnp.zeros((span, span), jnp.float32)
    for k in range(CAP // PAIR):
        block = reach_ref[k * span : (k + 1) * span, k * span : (k + 1) * span]
        mask = jnp.where(step == k, block, mask)
    mask = jnp.concatenate(
        [mask[s * nodes : (s + 1) * nodes] for s in range(PAIR) for h in range(heads)], axis=0
    )
    drafts = lax.dot_general(query, tree[:, :width], dims, preferred_element_type=jnp.float32)
    drafts = jnp.where(mask > 0, drafts, NEG)
    peak = jnp.max(drafts, axis=1, keepdims=True)
    drafts = (jnp.exp2((drafts - peak) * scale) * mask).astype(jnp.bfloat16)
    tree_value = jnp.concatenate([tree[:, width:], jnp.ones((span, width), jnp.bfloat16)], axis=1)
    peaks = [peak]
    sums = [jnp.dot(drafts, tree_value, preferred_element_type=jnp.float32)]
    for k, ref in enumerate((own_ref, other_ref)):
        scores = lax.dot_general(query, ref[:, :width], dims, preferred_element_type=jnp.float32)
        peak = jnp.max(scores, axis=1, keepdims=True)
        weights = jnp.exp2((scores - peak) * scale).astype(jnp.bfloat16)
        peaks.append(peak)
        sums.append(
            jnp.dot(
                weights, value_ref[pl.ds(k * half, half), :], preferred_element_type=jnp.float32
            )
        )
    top = jnp.maximum(jnp.maximum(peaks[0], peaks[1]), peaks[2])
    summed = sum(jnp.exp2((peak - top) * scale) * part for peak, part in zip(peaks, sums))
    attended = (summed[:, :width] / summed[:, width:]).astype(jnp.bfloat16)
    for s in range(PAIR):
        for h in range(heads):
            start = (s * heads + h) * nodes
            out_ref[s, :, h * width : (h + 1) * width] = attended[start : start + nodes]


def attend(slot, parents, picked, own, other):
    nodes, depth = picked.shape[1:]
    width = own.shape[1] // 2
    half = own.shape[0]
    model = depth - 2 * width
    return pl.pallas_call(
        attend_kernel,
        out_shape=jax.ShapeDtypeStruct((CAP, nodes, model), jnp.bfloat16),
        grid=(CAP // PAIR,),
        in_specs=[
            pl.BlockSpec(slot.shape, lambda i: (0, 0)),
            pl.BlockSpec(parents.shape, lambda i: (0, 0)),
            pl.BlockSpec((PAIR, nodes, depth), lambda i: (i, 0, 0)),
            pl.BlockSpec((half, 2 * width), lambda i: (0, 0)),
            pl.BlockSpec((half, 2 * width), lambda i: (0, 0)),
        ],
        out_specs=pl.BlockSpec((PAIR, nodes, model), lambda i: (i, 0, 0)),
        scratch_shapes=[
            pltpu.VMEM((CAP * nodes, CAP * nodes), jnp.float32),
            pltpu.VMEM((2 * half, 2 * width), jnp.bfloat16),
        ],
        compiler_params=pltpu.CompilerParams(vmem_limit_bytes=40 * 1024 * 1024),
        name="attend",
    )(slot, parents, picked, own, other)


def settle_kernel(source_ref, spread_ref, out_ref):
    for k in range(out_ref.shape[0]):
        out_ref[k] = encode(spread_ref[source_ref[0, k]].astype(jnp.float32))


def settle(source, spread, count):
    vmem = pl.BlockSpec(memory_space=pltpu.VMEM)
    return pl.pallas_call(
        settle_kernel,
        out_shape=jax.ShapeDtypeStruct((count, *spread.shape[1:]), jnp.float32),
        grid_spec=pltpu.PrefetchScalarGridSpec(
            num_scalar_prefetch=1, grid=(), in_specs=[vmem], out_specs=vmem
        ),
        compiler_params=pltpu.CompilerParams(vmem_limit_bytes=40 * 1024 * 1024),
        name="settle",
    )(source, spread)


def project_kernel(choice, spot_ref, every_ref, weight_ref, out_ref):
    lanes = out_ref.shape[0]
    share = spot_ref.shape[1] // lanes
    for lane in range(lanes):
        block = jnp.concatenate(
            [every_ref[spot_ref[choice, lane * share + r]] for r in range(share)], axis=0
        )
        out_ref[lane] = jnp.dot(
            block, weight_ref[...], preferred_element_type=jnp.float32
        ).astype(jnp.bfloat16)


def project(choice, spot, every, weight, lanes):
    requests, nodes = spot.shape[1], every.shape[1]
    columns = weight.shape[1]
    vmem = pl.BlockSpec(memory_space=pltpu.VMEM)
    return pl.pallas_call(
        functools.partial(project_kernel, choice),
        out_shape=jax.ShapeDtypeStruct((lanes, requests // lanes * nodes, columns), jnp.bfloat16),
        grid_spec=pltpu.PrefetchScalarGridSpec(
            num_scalar_prefetch=1, grid=(), in_specs=[vmem] * 2, out_specs=vmem
        ),
        compiler_params=pltpu.CompilerParams(vmem_limit_bytes=40 * 1024 * 1024),
        name="project",
    )(spot, every, weight)


def share_rows(choice, lanes, source, spread, spot, weight):
    settled = settle(source, spread, ROWS[choice])
    every = lax.all_gather(settled.astype(jnp.float16), "dp", axis=0, tiled=True)
    return project(choice, spot, decode(every), weight, lanes)


def local(queries, tree_kv, prefix_kv, request_holder, parents, out_weight):
    lanes = lax.axis_size("tensor")
    groups = lax.axis_size("dp")
    requests = request_holder.shape[0]
    nodes = queries.shape[1]
    own_half = prefix_kv[0, 0]
    other_half = swapped(own_half, "tensor", 0)
    packed, slot, index, spot, source, most = pack(queries, tree_kv, request_holder)
    packed = lax.all_gather(packed.astype(jnp.float16), "dp", axis=0, tiled=True)
    picked = decode(packed.at[index[0, :CAP]].get(mode="promise_in_bounds"))
    attended = attend(slot, parents, picked, own_half, other_half)
    blocks = [list(range(i, i + BLOCK)) for i in range(0, groups, BLOCK)]
    spread = lax.all_to_all(attended, "dp", 0, 0, axis_index_groups=blocks, tiled=True)
    partial = lax.switch(
        most[0, 0],
        [functools.partial(share_rows, choice, lanes) for choice in range(len(ROWS))],
        source,
        spread,
        spot,
        out_weight,
    )
    shares = lax.all_to_all(partial, "tensor", 0, 0, tiled=True)
    total = jnp.sum(shares.astype(jnp.float32), axis=0).astype(jnp.bfloat16)
    return total.reshape(requests // lanes, nodes, out_weight.shape[1])


def solution(mesh):
    return jax.shard_map(
        local,
        mesh=mesh,
        in_specs=(
            P("dp", None, "tensor"),
            P("dp", None, None, None),
            P("dp", "tensor", None, None),
            P(),
            P(),
            P("tensor", "dp"),
        ),
        out_specs=P("tensor", None, "dp"),
        check_vma=False,
    )
```

time: 244 us -> 192 us (0.79)
  waiting for transfers between devices: 103 us -> 14.5 us
  blocking collectives: 91.2 us -> 142 us
  between operations: 13.5 us -> 0.11 us
  Pallas kernels: 24.6 us -> 13 us
  other arithmetic: 1.17 us -> 5.88 us
  starting transfers between devices: 4.16 us -> 7.56 us
    all_gather x1 -> x0, waiting for transfers between devices: 103 us -> none  [local(): every = lax.all_gather(attended, 'dp', axis=0, tiled=True)]
    all_gather x0 -> x1, blocking collectives: none -> 52.5 us  [share_rows(): lax.all_gather(settled.astype(jnp.float16), 'dp', axis=0, tiled=True)]
    all_to_all x0 -> x1, waiting for transfers between devices: none -> 14.5 us  [local(): lax.all_to_all(attended, 'dp', 0, 0, axis_index_groups=blocks, tiled=True)]
    pallas_call x1, Pallas kernels: 15.8 us -> 8.33 us  [attend(): pl.pallas_call(attend_kernel, out_shape=jax.ShapeDtypeStruct((CAP, nodes,...]
    pallas_call x1 -> x2, Pallas kernels: 7.86 us -> 3.73 us  [the longest x1 2.92 us: project(): pl.pallas_call(functools.partial(project_kernel, choice), out_shape=jax.S...]
    all_to_all x0 -> x1, starting transfers between devices: none -> 3.54 us  [local(): lax.all_to_all(attended, 'dp', 0, 0, axis_index_groups=blocks, tiled=True)]
    convert_element_type x1 -> x3, other arithmetic: 0.09 us -> 3.28 us  [the longest x2 3.26 us: decode(): return (x * jnp.abs(x) * (x * (1.0 / LIFT) * x)).astype(jnp.bfloat16)]
  transfers between devices with their start and end apart: 2 -> 2, of which waited for: 1 -> 1; matrix products, arithmetic and copies ran while one was open for 2% -> 2% of each run, Pallas kernels for 0% -> 1%
where the time goes in v5:
time: 192 us; the launch traced here: 191 us
  blocking collectives  142 us (74%)
  waiting for transfers between devices  14.5 us (8%)
  Pallas kernels  13 us (7%)
  local copies, waits for them, and re-layouts  7.66 us (4%)
  starting transfers between devices  7.56 us (4%)
  other arithmetic  5.88 us (3%)
    all_gather x1, blocking collectives, local(): lax.all_gather(packed.astype(jnp.float16), 'dp', axis=0, tiled=True)  56 us
    all_gather x1, blocking collectives, share_rows(): lax.all_gather(settled.astype(jnp.float16), 'dp', axis=0, tiled=True)  52.5 us
    all_to_all x1, blocking collectives, local(): shares = lax.all_to_all(partial, 'tensor', 0, 0, tiled=True)  33.4 us
    all_to_all x1, waiting for transfers between devices, local(): lax.all_to_all(attended, 'dp', 0, 0, axis_index_groups=blocks, tiled=True)  14.5 us
    pallas_call x1, Pallas kernels, attend(): pl.pallas_call(attend_kernel, out_shape=jax.ShapeDtypeStruct((CAP, nodes,...  8.33 us
    unnamed x9, local copies, waits for them, and re-layouts  4.33 us
    ppermute x1, starting transfers between devices, swapped(): lax.ppermute(x, axis, [(i, i ^ 1 << bit) for i in range(lax.axis_size(axi...  4.02 us
  transfers between devices with their start and end apart: 2, of which 1 were waited for; matrix products, arithmetic and copies ran while one was open for 2% of the time, Pallas kernels for 1%

profile of v5, /device:TPU:1, one launch (start us, length us, event | category | flops | bytes accessed | tf_op | source)
XLA Modules:
  0.0 191.2 jit_solution(18032368604966727737)
XLA Ops:
  0.0 4.0 %collective-permute-start = (bf16[1024,256]{1,0:T(8,128)(2,1)}, bf16[1024,256]{1,0:T(8,128)(2,1)S(1)}, u32[]{:S(2)}, u32[]{:S(2)}) collective-permute-start(bf16[1024,256]{1,0:T(8,128)(2,1)} %bitcast.9), channel_id=1, source_target_pairs={{0,1},{1,0},{2,3},{3,2},{4,5},{5,4},{6,7},{7,6},{8,9},{9,8},{10,11... | collective-permute-start | bytes 1572872 | tf_op jit(solution)/shard_map/ppermute | solution.py:20
  4.0 0.0 copy-start.2
  4.0 0.9 copy-done.2
  5.0 0.0 copy-start.3
  5.0 0.9 copy-done.3
  5.9 0.0 copy-start.4
  5.9 0.7 copy-done.4
  6.5 1.0 pack.1
  7.5 56.0 %all-gather.9 = f16[128,16,1280]{2,1,0:T(8,128)(2,1)} all-gather(f16[4,16,1280]{2,1,0:T(8,128)(2,1)S(1)} %convert_element_type.47), channel_id=1, replica_groups=mesh['dp'=32,'tensor'=16] {'dp'}, dimensions={0}, use_global_device_ids=true | all-gather | bytes 5406720 | tf_op jit(solution)/shard_map/all_gather | solution.py:257
  63.5 0.8 copy.8.parents_ref
  64.3 3.3 %gather_fusion = f16[16,16,1280]{2,1,0:T(8,128)(2,1)S(1)} fusion(f16[128,16,1280]{2,1,0:T(8,128)(2,1)} %all-gather.9, s32[1024]{0:T(1024)S(1)} %pad_clamp_fusion), kind=kCustom, calls=%fused_computation | custom fusion | bytes 1310784 | tf_op jit(solution)/shard_map/gather | solution.py:258
  67.7 0.3 fusion.9.picked_ref
  67.9 0.0 collective-permute-done.other_ref
  68.0 0.0 copy-start.1
  68.0 1.0 copy-done.1
  69.0 8.3 %attend.1 = bf16[16,16,1024]{2,1,0:T(8,128)(2,1)} custom-call(s32[1,128]{1,0:T(1,128)S(1)} %get-tuple-element.66.slot_ref, s32[128,16]{1,0:T(8,128)S(1)} %copy.8.parents_ref, bf16[16,16,1280]{2,1,0:T(8,128)(2,1)S(1)} %fusion.9.picked_ref, bf16[1024,256]{1,0:T(8,128)(2,1)S(1)} %bitcast.10, bf16[1024,256]{1,0:T(8,128)(2,1)S(1)} %collective-permute-done.other_ref), custom_call_target="tpu_custom_call" | custom-call | tf_op jit(solution)/shard_map/attend/pallas_call | solution.py:177
  77.3 3.5 %all-to-all-start = ((bf16[16,16,1024]{2,1,0:T(8,128)(2,1)}), bf16[16,16,1024]{2,1,0:T(8,128)(2,1)S(1)}, u32[]{:S(2)}, u32[]{:S(2)}) async-start(bf16[16,16,1024]{2,1,0:T(8,128)(2,1)} %attend.1), calls=%async_computation | async-start | bytes 1048576 | tf_op jit(solution)/shard_map/all_to_all | solution.py:261
  80.9 14.5 %all-to-all-done = bf16[16,16,1024]{2,1,0:T(8,128)(2,1)S(1)} async-done(((bf16[16,16,1024]{2,1,0:T(8,128)(2,1)}), bf16[16,16,1024]{2,1,0:T(8,128)(2,1)S(1)}, u32[]{:S(2)}, u32[]{:S(2)}) %all-to-all-start) | async-done | bytes 524320 | tf_op jit(solution)/shard_map/all_to_all | solution.py:261
  95.4 59.8 %conditional.1 = (bf16[16,128,512]{2,1,0:T(8,128)(2,1)S(1)}) conditional(s32[]{:T(128)} %bitcast.1, (s32[1,128]{1,0:T(1,128)S(1)}, bf16[16,16,1024]{2,1,0:T(8,128)(2,1)S(1)}, s32[4,128]{1,0:T(4,128)S(1)}, bf16[1024,512]{1,0:T(8,128)(2,1)}) %tuple.17, (s32[1,128]{1,0:T(1,128)S(1)}, ...), branch_computations={%region_0.0_spmd, %region_1.0_spmd, %region_2.0_spmd, %region_3.0_... | conditional | flops 58982400 | bytes 63963200 | solution.py:262
  95.4 0.0 copy-start.5
  95.4 0.8 settle.4
  96.2 52.5 %all-gather.5 = f16[192,16,1024]{2,1,0:T(8,128)(2,1)S(1)} all-gather(f16[6,16,1024]{2,1,0:T(8,128)(2,1)S(1)} %convert_element_type.22), channel_id=1, replica_groups=mesh['dp'=32,'tensor'=16] {'dp'}, dimensions={0}, use_global_device_ids=true | all-gather | bytes 6488064 | tf_op jit(solution)/shard_map/cond/branch_0_fun/all_gather | solution.py:245
  148.7 3.0 %fusion.1.every_ref = bf16[192,16,1024]{2,1,0:T(8,128)(2,1)S(1)} fusion(f16[192,16,1024]{2,1,0:T(8,128)(2,1)S(1)} %all-gather.5), kind=kLoop, calls=%fused_computation.6 | loop fusion | flops 22020096 | bytes 12582912 | tf_op jit(solution)/shard_map/cond/branch_0_fun/convert_element_type | solution.py:30
  151.7 0.0 copy-done.5
  151.7 2.9 %project.4 = bf16[16,128,512]{2,1,0:T(8,128)(2,1)S(1)} custom-call(s32[4,128]{1,0:T(4,128)S(1)} %get-tuple-element.40.spot_ref, bf16[192,16,1024]{2,1,0:T(8,128)(2,1)S(1)} %fusion.1.every_ref, bf16[1024,512]{1,0:T(8,128)(2,1)S(1)} %copy-done.5), custom_call_target="tpu_custom_call" | custom-call | tf_op jit(solution)/shard_map/cond/branch_0_fun/project/pallas_call | solution.py:232
  155.2 33.4 %all_to_all.10 = bf16[16,128,512]{2,1,0:T(8,128)(2,1)} all-to-all(bf16[16,128,512]{2,1,0:T(8,128)(2,1)S(1)} %get-tuple-element.70), channel_id=1, replica_groups=mesh['dp'=32,'tensor'=16] {'tensor'}, dimensions={0} | all-to-all | bytes 4194304 | tf_op jit(solution)/shard_map/all_to_all | solution.py:270
  188.6 2.6 %reduce_sum.12 = bf16[128,512]{1,0:T(8,128)(2,1)} reduce(bf16[16,128,512]{2,1,0:T(8,128)(2,1)} %all_to_all.10, bf16[]{:T(256)} %constant.22.clone.1), dimensions={0}, to_apply=%region_4.0 | reduce | flops 983040 | bytes 2228226 | tf_op jit(solution)/shard_map/reduce_sum | solution.py:271
  (4 shorter events, 0.1 us)
Async XLA Ops:
  0.0 67.9 %collective-permute-start = (bf16[1024,256]{1,0:T(8,128)(2,1)}, bf16[1024,256]{1,0:T(8,128)(2,1)S(1)}, u32[]{:S(2)}, u32[]{:S(2)}) collective-permute-start(bf16[1024,256]{1,0:T(8,128)(2,1)} %bitcast.9), channel_id=1, source_target_pairs={{0,1},{1,0},{2,3},{3,2},{4,5},{5,4},{6,7},{7,6},{8,9},{9,8},{10,11... | collective-permute-start | bytes 1572872 | tf_op jit(solution)/shard_map/ppermute | solution.py:20
  4.0 1.0 copy-start.2
  5.0 0.9 copy-start.3
  5.9 0.7 copy-start.4
  68.0 1.0 copy-start.1
  77.3 18.0 %all-to-all-start = ((bf16[16,16,1024]{2,1,0:T(8,128)(2,1)}), bf16[16,16,1024]{2,1,0:T(8,128)(2,1)S(1)}, u32[]{:S(2)}, u32[]{:S(2)}) async-start(bf16[16,16,1024]{2,1,0:T(8,128)(2,1)} %attend.1), calls=%async_computation | async-start | bytes 1048576 | tf_op jit(solution)/shard_map/all_to_all | solution.py:261
  95.4 56.4 %copy-start.5 = (bf16[1024,512]{1,0:T(8,128)(2,1)S(1)}, bf16[1024,512]{1,0:T(8,128)(2,1)}, u32[]{:S(2)}) copy-start(bf16[1024,512]{1,0:T(8,128)(2,1)} %get-tuple-element.45.weight_ref) | copy-start | bytes 3145732 | tf_op jit(solution)/shard_map/cond

commit v6 on v5

--- a/solution.py
+++ b/solution.py
@@ -90,7 +90,7 @@
         ),
         in_specs=[vmem] * 3,
         out_specs=(vmem,) * 6,
-        compiler_params=pltpu.CompilerParams(vmem_limit_bytes=40 * 1024 * 1024),
+        compiler_params=pltpu.CompilerParams(vmem_limit_bytes=8 * 1024 * 1024),
         name="pack",
     )(queries, tree, holder.reshape(1, requests))
 
@@ -109,9 +109,10 @@
         column = lax.broadcasted_iota(jnp.int32, (rows, rows), 1)
         requests = slot_ref.shape[1]
         taken = lax.broadcasted_iota(jnp.int32, (rows, requests), 0) // nodes == slot_ref[...]
-        above = jnp.dot(
+        above = lax.dot_general(
             jnp.where(taken, 1.0, 0.0).astype(jnp.bfloat16),
             parents_ref[...].astype(jnp.float32).astype(jnp.bfloat16),
+            (((1,), (1,)), ((), ())),
             preferred_element_type=jnp.float32,
         )
         node = lax.broadcasted_iota(jnp.int32, (rows, nodes), 0) % nodes
@@ -190,7 +191,7 @@
             pltpu.VMEM((CAP * nodes, CAP * nodes), jnp.float32),
             pltpu.VMEM((2 * half, 2 * width), jnp.bfloat16),
         ],
-        compiler_params=pltpu.CompilerParams(vmem_limit_bytes=40 * 1024 * 1024),
+        compiler_params=pltpu.CompilerParams(vmem_limit_bytes=24 * 1024 * 1024),
         name="attend",
     )(slot, parents, picked, own, other)
 
@@ -208,7 +209,7 @@
         grid_spec=pltpu.PrefetchScalarGridSpec(
             num_scalar_prefetch=1, grid=(), in_specs=[vmem], out_specs=vmem
         ),
-        compiler_params=pltpu.CompilerParams(vmem_limit_bytes=40 * 1024 * 1024),
+        compiler_params=pltpu.CompilerParams(vmem_limit_bytes=12 * 1024 * 1024),
         name="settle",
     )(source, spread)
 
@@ -235,7 +236,7 @@
         grid_spec=pltpu.PrefetchScalarGridSpec(
             num_scalar_prefetch=1, grid=(), in_specs=[vmem] * 2, out_specs=vmem
         ),
-        compiler_params=pltpu.CompilerParams(vmem_limit_bytes=40 * 1024 * 1024),
+        compiler_params=pltpu.CompilerParams(vmem_limit_bytes=16 * 1024 * 1024),
         name="project",
     )(spot, every, weight)
 
@@ -256,7 +257,7 @@
     packed, slot, index, spot, source, most = pack(queries, tree_kv, request_holder)
     packed = lax.all_gather(packed.astype(jnp.float16), "dp", axis=0, tiled=True)
     picked = decode(packed.at[index[0, :CAP]].get(mode="promise_in_bounds"))
-    attended = attend(slot, parents, picked, own_half, other_half)
+    attended = attend(slot, parents.T, picked, own_half, other_half)
     blocks = [list(range(i, i + BLOCK)) for i in range(0, groups, BLOCK)]
     spread = lax.all_to_all(attended, "dp", 0, 0, axis_index_groups=blocks, tiled=True)
     partial = lax.switch(

time: 192 us -> 201 us (1.047)
  blocking collectives: 142 us -> 147 us
  other arithmetic: 5.88 us -> 9.47 us
    all_gather x1, blocking collectives: 52.5 us -> 57.9 us  [share_rows(): lax.all_gather(settled.astype(jnp.float16), 'dp', axis=0, tiled=True)]
    convert_element_type x2, other arithmetic: 3.26 us -> 6.84 us  [decode(): return (x * jnp.abs(x) * (x * (1.0 / LIFT) * x)).astype(jnp.bfloat16)]
    unnamed x9 -> x10, local copies, waits for them, and re-layouts: 4.33 us -> 4.23 us
  transfers between devices with their start and end apart: 2 -> 2, of which waited for: 1 -> 1; matrix products, arithmetic and copies ran while one was open for 2% -> 2% of each run, Pallas kernels for 1% -> 0%
where the time goes in v6:
time: 201 us; the launch traced here: 200 us
  blocking collectives  147 us (73%)
  waiting for transfers between devices  14.5 us (7%)
  Pallas kernels  13.8 us (7%)
  other arithmetic  9.47 us (5%)
  starting transfers between devices  7.56 us (4%)
  local copies, waits for them, and re-layouts  7.56 us (4%)
    all_gather x1, blocking collectives, share_rows(): lax.all_gather(settled.astype(jnp.float16), 'dp', axis=0, tiled=True)  57.9 us
    all_gather x1, blocking collectives, local(): lax.all_gather(packed.astype(jnp.float16), 'dp', axis=0, tiled=True)  56 us
    all_to_all x1, blocking collectives, local(): shares = lax.all_to_all(partial, 'tensor', 0, 0, tiled=True)  33.4 us
    all_to_all x1, waiting for transfers between devices, local(): lax.all_to_all(attended, 'dp', 0, 0, axis_index_groups=blocks, tiled=True)  14.5 us
    pallas_call x1, Pallas kernels, attend(): pl.pallas_call(attend_kernel, out_shape=jax.ShapeDtypeStruct((CAP, nodes,...  9.04 us
    convert_element_type x2, other arithmetic, decode(): return (x * jnp.abs(x) * (x * (1.0 / LIFT) * x)).astype(jnp.bfloat16)  6.84 us
    unnamed x10, local copies, waits for them, and re-layouts  4.23 us
    ppermute x1, starting transfers between devices, swapped(): lax.ppermute(x, axis, [(i, i ^ 1 << bit) for i in range(lax.axis_size(axi...  4.02 us
  transfers between devices with their start and end apart: 2, of which 1 were waited for; matrix products, arithmetic and copies ran while one was open for 2% of the time, Pallas kernels for 0%

profile of v6, /device:TPU:1, one launch (start us, length us, event | category | flops | bytes accessed | tf_op | source)
XLA Modules:
  0.0 200.5 jit_solution(5812109959939634713)
XLA Ops:
  0.0 4.0 %collective-permute-start = (bf16[1024,256]{1,0:T(8,128)(2,1)}, bf16[1024,256]{1,0:T(8,128)(2,1)S(1)}, u32[]{:S(2)}, u32[]{:S(2)}) collective-permute-start(bf16[1024,256]{1,0:T(8,128)(2,1)} %bitcast.10), channel_id=1, source_target_pairs={{0,1},{1,0},{2,3},{3,2},{4,5},{5,4},{6,7},{7,6},{8,9},{9,8},{10,11... | collective-permute-start | bytes 1572872 | tf_op jit(solution)/shard_map/ppermute | solution.py:20
  4.0 0.0 copy-start.2
  4.0 0.9 copy-done.2
  5.0 0.0 copy-start.3
  5.0 0.9 copy-done.3
  5.9 0.0 copy-start.5
  5.9 0.7 copy-done.5
  6.5 1.0 pack.1
  7.5 56.0 %all-gather.9 = f16[128,16,1280]{2,1,0:T(8,128)(2,1)} all-gather(f16[4,16,1280]{2,1,0:T(8,128)(2,1)S(1)} %convert_element_type.47), channel_id=1, replica_groups=mesh['dp'=32,'tensor'=16] {'dp'}, dimensions={0}, use_global_device_ids=true | all-gather | bytes 5406720 | tf_op jit(solution)/shard_map/all_gather | solution.py:258
  63.5 3.3 %gather_fusion = f16[16,16,1280]{2,1,0:T(8,128)(2,1)S(1)} fusion(f16[128,16,1280]{2,1,0:T(8,128)(2,1)} %all-gather.9, s32[1024]{0:T(1024)S(1)} %pad_clamp_fusion), kind=kCustom, calls=%fused_computation | custom fusion | bytes 1310784 | tf_op jit(solution)/shard_map/gather | solution.py:259
  66.9 0.3 fusion.9.picked_ref
  67.1 0.0 collective-permute-done.other_ref
  67.2 0.0 copy-start.1
  67.2 1.0 copy-done.1
  68.2 0.0 copy-start.4
  68.2 0.7 copy-done.4
  68.9 9.0 %attend.1 = bf16[16,16,1024]{2,1,0:T(8,128)(2,1)} custom-call(s32[1,128]{1,0:T(1,128)S(1)} %get-tuple-element.66.slot_ref, s32[16,128]{1,0:T(8,128)S(1)} %bitcast.12, bf16[16,16,1280]{2,1,0:T(8,128)(2,1)S(1)} %fusion.9.picked_ref, bf16[1024,256]{1,0:T(8,128)(2,1)S(1)} %bitcast.11, bf16[1024,256]{1,0:T(8,128)(2,1)S(1)} %collective-permute-done.other_ref), custom_call_target="tpu_custom_call" | custom-call | tf_op jit(solution)/shard_map/attend/pallas_call | solution.py:178
  77.9 3.5 %all-to-all-start = ((bf16[16,16,1024]{2,1,0:T(8,128)(2,1)}), bf16[16,16,1024]{2,1,0:T(8,128)(2,1)S(1)}, u32[]{:S(2)}, u32[]{:S(2)}) async-start(bf16[16,16,1024]{2,1,0:T(8,128)(2,1)} %attend.1), calls=%async_computation | async-start | bytes 1048576 | tf_op jit(solution)/shard_map/all_to_all | solution.py:262
  81.5 14.5 %all-to-all-done = bf16[16,16,1024]{2,1,0:T(8,128)(2,1)S(1)} async-done(((bf16[16,16,1024]{2,1,0:T(8,128)(2,1)}), bf16[16,16,1024]{2,1,0:T(8,128)(2,1)S(1)}, u32[]{:S(2)}, u32[]{:S(2)}) %all-to-all-start) | async-done | bytes 524320 | tf_op jit(solution)/shard_map/all_to_all | solution.py:262
  96.0 68.5 %conditional.1 = (bf16[16,128,512]{2,1,0:T(8,128)(2,1)S(1)}) conditional(s32[]{:T(128)} %bitcast.1, (s32[1,128]{1,0:T(1,128)S(1)}, bf16[16,16,1024]{2,1,0:T(8,128)(2,1)S(1)}, s32[4,128]{1,0:T(4,128)S(1)}, bf16[1024,512]{1,0:T(8,128)(2,1)}) %tuple.17, (s32[1,128]{1,0:T(1,128)S(1)}, ...), branch_computations={%region_0.0_spmd, %region_1.0_spmd, %region_2.0_spmd, %region_3.0_... | conditional | flops 58982400 | bytes 63963200 | solution.py:263
  96.0 0.0 copy-start.7
  96.0 0.8 settle.5
  96.9 57.9 %all-gather.6 = f16[224,16,1024]{2,1,0:T(8,128)(2,1)} all-gather(f16[7,16,1024]{2,1,0:T(8,128)(2,1)S(1)} %convert_element_type.35), channel_id=1, replica_groups=mesh['dp'=32,'tensor'=16] {'dp'}, dimensions={0}, use_global_device_ids=true | all-gather | bytes 7569408 | tf_op jit(solution)/shard_map/cond/branch_1_fun/all_gather | solution.py:246
  154.8 6.6 %fusion.3.every_ref = bf16[224,16,1024]{2,1,0:T(8,128)(2,1)S(1)} fusion(f16[224,16,1024]{2,1,0:T(8,128)(2,1)} %all-gather.6), kind=kLoop, calls=%fused_computation.12 | loop fusion | flops 25690112 | bytes 14680064 | tf_op jit(solution)/shard_map/cond/branch_1_fun/convert_element_type | solution.py:30
  161.3 0.0 copy-done.7
  161.3 2.9 %project.5 = bf16[16,128,512]{2,1,0:T(8,128)(2,1)S(1)} custom-call(s32[4,128]{1,0:T(4,128)S(1)} %get-tuple-element.46.spot_ref, bf16[224,16,1024]{2,1,0:T(8,128)(2,1)S(1)} %fusion.3.every_ref, bf16[1024,512]{1,0:T(8,128)(2,1)S(1)} %copy-done.7), custom_call_target="tpu_custom_call" | custom-call | tf_op jit(solution)/shard_map/cond/branch_1_fun/project/pallas_call | solution.py:233
  164.5 33.4 %all_to_all.10 = bf16[16,128,512]{2,1,0:T(8,128)(2,1)} all-to-all(bf16[16,128,512]{2,1,0:T(8,128)(2,1)S(1)} %get-tuple-element.70), channel_id=1, replica_groups=mesh['dp'=32,'tensor'=16] {'tensor'}, dimensions={0} | all-to-all | bytes 4194304 | tf_op jit(solution)/shard_map/all_to_all | solution.py:271
  197.9 2.6 %reduce_sum.12 = bf16[128,512]{1,0:T(8,128)(2,1)} reduce(bf16[16,128,512]{2,1,0:T(8,128)(2,1)} %all_to_all.10, bf16[]{:T(256)} %constant.22.clone.1), dimensions={0}, to_apply=%region_4.0 | reduce | flops 983040 | bytes 2228226 | tf_op jit(solution)/shard_map/reduce_sum | solution.py:272
  (4 shorter events, 0.1 us)
Async XLA Ops:
  0.0 67.1 %collective-permute-start = (bf16[1024,256]{1,0:T(8,128)(2,1)}, bf16[1024,256]{1,0:T(8,128)(2,1)S(1)}, u32[]{:S(2)}, u32[]{:S(2)}) collective-permute-start(bf16[1024,256]{1,0:T(8,128)(2,1)} %bitcast.10), channel_id=1, source_target_pairs={{0,1},{1,0},{2,3},{3,2},{4,5},{5,4},{6,7},{7,6},{8,9},{9,8},{10,11... | collective-permute-start | bytes 1572872 | tf_op jit(solution)/shard_map/ppermute | solution.py:20
  4.0 1.0 copy-start.2
  5.0 0.9 copy-start.3
  5.9 0.7 copy-start.5
  67.2 1.0 copy-start.1
  68.2 0.7 copy-start.4
  77.9 18.0 %all-to-all-start = ((bf16[16,16,1024]{2,1,0:T(8,128)(2,1)}), bf16[16,16,1024]{2,1,0:T(8,128)(2,1)S(1)}, u32[]{:S(2)}, u32[]{:S(2)}) async-start(bf16[16,16,1024]{2,1,0:T(8,128)(2,1)} %attend.1), calls=%async_computation | async-start | bytes 1048576 | tf_op jit(solution)/shard_map/all_to_all | solution.py:262
  96.0 65.4 %copy-start.7 = (bf16[1024,512]{1,0:T(8,128)(2,1)S(1)}, bf16[1024,512]{1,0:T(8,128)(2,1)}, u32[]{:S(2)}) copy-start(bf16[1024,512]{1,0:T(8,128)(2,1)} %get-tuple-element.49.weight_ref) | copy-start | bytes 3145732 | tf_op jit(solution)/shard_map/cond

commit v7 on v6

--- a/solution.py
+++ b/solution.py
@@ -11,13 +11,20 @@
 CAP = 16
 PAIR = 16
 BLOCK = 8
-ROWS = (6, 7, 8, 16)
+ROWS = (6, 8, 16)
+QUAD = 4
 NEG = -1e30
 LIFT = 2.0**59
 
 
 def swapped(x, axis, bit):
     return lax.ppermute(x, axis, [(i, i ^ 1 << bit) for i in range(lax.axis_size(axis))])
+
+
+def turned(x, by):
+    lanes = lax.axis_size("tensor")
+    pairs = [(i - i % QUAD + (i + by) % QUAD, i) for i in range(lanes)]
+    return lax.ppermute(x, "tensor", pairs)
 
 
 def encode(x):
@@ -196,16 +203,33 @@
     )(slot, parents, picked, own, other)
 
 
+def interleave(first, second, swap):
+    lower = lax.broadcasted_iota(jnp.int32, first.shape, 0) < QUAD
+    if swap:
+        return jnp.where(lower, pltpu.roll(first, QUAD, 0), second)
+    return jnp.where(lower, first, pltpu.roll(second, QUAD, 0))
+
+
 def settle_kernel(source_ref, spread_ref, out_ref):
-    for k in range(out_ref.shape[0]):
-        out_ref[k] = encode(spread_ref[source_ref[0, k]].astype(jnp.float32))
+    count = out_ref.shape[1] // QUAD
+    tiles = [[] for _ in range(QUAD)]
+    for k in range(0, count, 2):
+        first = spread_ref[source_ref[0, k]].astype(jnp.float32)
+        second = spread_ref[source_ref[0, k + 1]].astype(jnp.float32)
+        for quarter in range(QUAD):
+            at = quarter // 2 * 8
+            tiles[quarter].append(
+                interleave(first[at : at + 8], second[at : at + 8], quarter % 2 == 1)
+            )
+    for quarter in range(QUAD):
+        out_ref[quarter] = jnp.concatenate(tiles[quarter], axis=0).astype(jnp.bfloat16)
 
 
 def settle(source, spread, count):
     vmem = pl.BlockSpec(memory_space=pltpu.VMEM)
     return pl.pallas_call(
         settle_kernel,
-        out_shape=jax.ShapeDtypeStruct((count, *spread.shape[1:]), jnp.float32),
+        out_shape=jax.ShapeDtypeStruct((QUAD, count * QUAD, spread.shape[2]), jnp.bfloat16),
         grid_spec=pltpu.PrefetchScalarGridSpec(
             num_scalar_prefetch=1, grid=(), in_specs=[vmem], out_specs=vmem
         ),
@@ -214,37 +238,107 @@
     )(source, spread)
 
 
-def project_kernel(choice, spot_ref, every_ref, weight_ref, out_ref):
-    lanes = out_ref.shape[0]
-    share = spot_ref.shape[1] // lanes
-    for lane in range(lanes):
-        block = jnp.concatenate(
-            [every_ref[spot_ref[choice, lane * share + r]] for r in range(share)], axis=0
-        )
-        out_ref[lane] = jnp.dot(
-            block, weight_ref[...], preferred_element_type=jnp.float32
+def join_kernel(quarters_ref, out_ref):
+    depth = quarters_ref.shape[2]
+    lane = lax.axis_index("tensor")
+    for k in range(QUAD):
+        part = quarters_ref[(lane + k) & (QUAD - 1)].astype(jnp.float32)
+        out_ref[:, k * depth : (k + 1) * depth] = encode(part)
+
+
+def join(quarters):
+    vmem = pl.BlockSpec(memory_space=pltpu.VMEM)
+    rows, depth = quarters.shape[1:]
+    return pl.pallas_call(
+        join_kernel,
+        out_shape=jax.ShapeDtypeStruct((rows, QUAD * depth), jnp.float32),
+        in_specs=[vmem],
+        out_specs=vmem,
+        compiler_params=pltpu.CompilerParams(vmem_limit_bytes=12 * 1024 * 1024),
+        name="join",
+    )(quarters)
+
+
+def project_kernel(choice, spot_ref, every_ref, *refs):
+    weight_refs, out_ref, sum_ref = refs[:QUAD], refs[QUAD], refs[QUAD + 1]
+    depth = weight_refs[0].shape[0]
+    requests = spot_ref.shape[1]
+    count = requests * QUAD
+    line = lax.broadcasted_iota(jnp.int32, (count, requests), 0)
+    lane = lax.broadcasted_iota(jnp.int32, (count, requests), 1)
+    spots = jnp.broadcast_to(spot_ref[choice : choice + 1, :], (count, requests))
+    wanted = jnp.sum(jnp.where((line >> 2) == lane, spots, 0), axis=1, keepdims=True) * QUAD
+    wanted = wanted + (lax.broadcasted_iota(jnp.int32, (count, 1), 0) & (QUAD - 1))
+    step = 256
+    for start in range(0, every_ref.shape[0], step):
+        product = sum(
+            jnp.dot(
+                every_ref[start : start + step, k * depth : (k + 1) * depth],
+                ref[...],
+                preferred_element_type=jnp.float32,
+            )
+            for k, ref in enumerate(weight_refs)
         ).astype(jnp.bfloat16)
-
-
-def project(choice, spot, every, weight, lanes):
-    requests, nodes = spot.shape[1], every.shape[1]
-    columns = weight.shape[1]
+        column = lax.broadcasted_iota(jnp.int32, (count, step), 1) + start
+        chosen = jnp.where(column == wanted, 1.0, 0.0).astype(jnp.bfloat16)
+        moved = jnp.dot(chosen, product, preferred_element_type=jnp.float32)
+        if start == 0:
+            sum_ref[...] = moved
+        else:
+            sum_ref[...] += moved
+    out_ref[...] = sum_ref[...].astype(jnp.bfloat16)
+
+
+def project(choice, spot, every, weights):
+    requests = spot.shape[1]
+    columns = weights[0].shape[1]
     vmem = pl.BlockSpec(memory_space=pltpu.VMEM)
     return pl.pallas_call(
         functools.partial(project_kernel, choice),
-        out_shape=jax.ShapeDtypeStruct((lanes, requests // lanes * nodes, columns), jnp.bfloat16),
-        grid_spec=pltpu.PrefetchScalarGridSpec(
-            num_scalar_prefetch=1, grid=(), in_specs=[vmem] * 2, out_specs=vmem
-        ),
-        compiler_params=pltpu.CompilerParams(vmem_limit_bytes=16 * 1024 * 1024),
+        out_shape=jax.ShapeDtypeStruct((requests * QUAD, columns), jnp.bfloat16),
+        in_specs=[vmem] * (2 + QUAD),
+        out_specs=vmem,
+        scratch_shapes=[pltpu.VMEM((requests * QUAD, columns), jnp.float32)],
+        compiler_params=pltpu.CompilerParams(vmem_limit_bytes=32 * 1024 * 1024),
         name="project",
-    )(spot, every, weight)
-
-
-def share_rows(choice, lanes, source, spread, spot, weight):
-    settled = settle(source, spread, ROWS[choice])
-    every = lax.all_gather(settled.astype(jnp.float16), "dp", axis=0, tiled=True)
-    return project(choice, spot, decode(every), weight, lanes)
+    )(spot, every, *weights)
+
+
+def finish_kernel(shares_ref, out_ref):
+    requests = out_ref.shape[0]
+    lanes = shares_ref.shape[0]
+    quarters = [
+        sum(shares_ref[lane].astype(jnp.float32) for lane in range(quarter, lanes, QUAD))
+        for quarter in range(QUAD)
+    ]
+    for r in range(requests):
+        at = r // 2 * 8
+        tiles = [
+            interleave(quarters[k][at : at + 8], quarters[k + 1][at : at + 8], r % 2 == 1)
+            for k in range(0, QUAD, 2)
+        ]
+        out_ref[r] = jnp.concatenate(tiles, axis=0).astype(jnp.bfloat16)
+
+
+def finish(shares, nodes):
+    rows, columns = shares.shape[1:]
+    vmem = pl.BlockSpec(memory_space=pltpu.VMEM)
+    return pl.pallas_call(
+        finish_kernel,
+        out_shape=jax.ShapeDtypeStruct((rows // QUAD, nodes, columns), jnp.bfloat16),
+        in_specs=[vmem],
+        out_specs=vmem,
+        compiler_params=pltpu.CompilerParams(vmem_limit_bytes=12 * 1024 * 1024),
+        name="finish",
+    )(shares)
+
+
+def share_rows(choice, quads, source, spread, spot, *weights):
+    quarters = settle(source, spread, ROWS[choice])
+    quarters = lax.all_to_all(quarters, "tensor", 0, 0, axis_index_groups=quads, tiled=True)
+    joined = join(quarters)
+    every = lax.all_gather(joined.astype(jnp.float16), "dp", axis=0, tiled=True)
+    return project(choice, spot, decode(every), weights)
 
 
 def local(queries, tree_kv, prefix_kv, request_holder, parents, out_weight):
@@ -255,22 +349,25 @@
     own_half = prefix_kv[0, 0]
     other_half = swapped(own_half, "tensor", 0)
     packed, slot, index, spot, source, most = pack(queries, tree_kv, request_holder)
+    packed, out_weight = lax.optimization_barrier((packed, out_weight))
+    weights = [out_weight] + [turned(out_weight, by) for by in range(1, QUAD)]
     packed = lax.all_gather(packed.astype(jnp.float16), "dp", axis=0, tiled=True)
     picked = decode(packed.at[index[0, :CAP]].get(mode="promise_in_bounds"))
     attended = attend(slot, parents.T, picked, own_half, other_half)
     blocks = [list(range(i, i + BLOCK)) for i in range(0, groups, BLOCK)]
     spread = lax.all_to_all(attended, "dp", 0, 0, axis_index_groups=blocks, tiled=True)
+    quads = [list(range(i, i + QUAD)) for i in range(0, lanes, QUAD)]
     partial = lax.switch(
         most[0, 0],
-        [functools.partial(share_rows, choice, lanes) for choice in range(len(ROWS))],
+        [functools.partial(share_rows, choice, quads) for choice in range(len(ROWS))],
         source,
         spread,
         spot,
-        out_weight,
+        *weights,
     )
+    partial = partial.reshape(lanes, requests // lanes * QUAD, out_weight.shape[1])
     shares = lax.all_to_all(partial, "tensor", 0, 0, tiled=True)
-    total = jnp.sum(shares.astype(jnp.float32), axis=0).astype(jnp.bfloat16)
-    return total.reshape(requests // lanes, nodes, out_weight.shape[1])
+    return finish(shares, nodes)
 
 
 def solution(mesh):

time: 201 us -> 228 us (1.13)
  waiting for transfers between devices: 14.5 us -> 42.2 us
  blocking collectives: 147 us -> 135 us
  starting transfers between devices: 7.56 us -> 18.6 us
  other arithmetic: 9.47 us -> 3.18 us
  Pallas kernels: 13.8 us -> 18.2 us
    ppermute x0 -> x3, waiting for transfers between devices: none -> 42.2 us  [turned(): return lax.ppermute(x, 'tensor', pairs)]
    all_to_all x1, blocking collectives: 33.4 us -> 14.7 us  [local(): shares = lax.all_to_all(partial, 'tensor', 0, 0, tiled=True)]
    all_to_all x1, waiting for transfers between devices: 14.5 us -> 0.01 us  [local(): lax.all_to_all(attended, 'dp', 0, 0, axis_index_groups=blocks, tiled=True)]
    ppermute x0 -> x3, starting transfers between devices: none -> 10.4 us  [turned(): return lax.ppermute(x, 'tensor', pairs)]
    all_to_all x0 -> x1, blocking collectives: none -> 9.39 us  [share_rows(): lax.all_to_all(quarters, 'tensor', 0, 0, axis_index_groups=quads, tiled=T...]
    convert_element_type x2, other arithmetic: 6.84 us -> 3.13 us  [decode(): return (x * jnp.abs(x) * (x * (1.0 / LIFT) * x)).astype(jnp.bfloat16)]
    all_gather x1, blocking collectives: 57.9 us -> 55.2 us  [share_rows(): every = lax.all_gather(joined.astype(jnp.float16), 'dp', axis=0, tiled=True)]
    reduce_sum x1 -> x0, other arithmetic: 2.57 us -> none  [local(): total = jnp.sum(shares.astype(jnp.float32), axis=0).astype(jnp.bfloat16)]
  transfers between devices with their start and end apart: 2 -> 5, of which waited for: 1 -> 3; matrix products, arithmetic and copies ran while one was open for 2% -> 2% of each run, Pallas kernels for 0% -> 0%
where the time goes in v7:
time: 228 us; the launch traced here: 226 us
  blocking collectives  135 us (59%)
  waiting for transfers between devices  42.2 us (19%)
  starting transfers between devices  18.6 us (8%)
  Pallas kernels  18.2 us (8%)
  local copies, waits for them, and re-layouts  7.56 us (3%)
  other arithmetic  3.18 us (1%)
    all_gather x1, blocking collectives, local(): lax.all_gather(packed.astype(jnp.float16), 'dp', axis=0, tiled=True)  56 us
    all_gather x1, blocking collectives, share_rows(): every = lax.all_gather(joined.astype(jnp.float16), 'dp', axis=0, tiled=True)  55.2 us
    ppermute x3, waiting for transfers between devices, turned(): return lax.ppermute(x, 'tensor', pairs)  42.2 us
    all_to_all x1, blocking collectives, local(): shares = lax.all_to_all(partial, 'tensor', 0, 0, tiled=True)  14.7 us
    ppermute x3, starting transfers between devices, turned(): return lax.ppermute(x, 'tensor', pairs)  10.4 us
    all_to_all x1, blocking collectives, share_rows(): lax.all_to_all(quarters, 'tensor', 0, 0, axis_index_groups=quads, tiled=T...  9.39 us
    pallas_call x1, Pallas kernels, attend(): pl.pallas_call(attend_kernel, out_shape=jax.ShapeDtypeStruct((CAP, nodes,...  9.13 us
    pallas_call x1, Pallas kernels, project(): pl.pallas_call(functools.partial(project_kernel, choice), out_shape=jax.S...  5.48 us
  transfers between devices with their start and end apart: 5, of which 3 were waited for; matrix products, arithmetic and copies ran while one was open for 2% of the time, Pallas kernels for 0%

profile of v7, /device:TPU:1, one launch (start us, length us, event | category | flops | bytes accessed | tf_op | source)
XLA Modules:
  0.0 225.8 jit_solution(18171204893646431403)
XLA Ops:
  0.0 4.0 %collective-permute-start = (bf16[1024,256]{1,0:T(8,128)(2,1)}, bf16[1024,256]{1,0:T(8,128)(2,1)S(1)}, u32[]{:S(2)}, u32[]{:S(2)}) collective-permute-start(bf16[1024,256]{1,0:T(8,128)(2,1)} %bitcast.10), channel_id=1, source_target_pairs={{0,1},{1,0},{2,3},{3,2},{4,5},{5,4},{6,7},{7,6},{8,9},{9,8},{10,11... | collective-permute-start | bytes 1572872 | tf_op jit(solution)/shard_map/ppermute | solution.py:21
  4.0 0.0 copy-start.2
  4.0 0.9 copy-done.2
  5.0 0.0 copy-start.3
  5.0 0.9 copy-done.3
  5.9 0.0 copy-start.5
  5.9 0.7 copy-done.5
  6.5 1.0 pack.1
  7.6 56.0 %all-gather.7 = f16[128,16,1280]{2,1,0:T(8,128)(2,1)} all-gather(f16[4,16,1280]{2,1,0:T(8,128)(2,1)S(1)} %convert_element_type.36), channel_id=1, replica_groups=mesh['dp'=32,'tensor'=16] {'dp'}, dimensions={0}, use_global_device_ids=true | all-gather | bytes 5406720 | tf_op jit(solution)/shard_map/all_gather | solution.py:354
  63.5 3.3 %gather_fusion = f16[16,16,1280]{2,1,0:T(8,128)(2,1)S(1)} fusion(f16[128,16,1280]{2,1,0:T(8,128)(2,1)} %all-gather.7, s32[1024]{0:T(1024)S(1)} %pad_clamp_fusion), kind=kCustom, calls=%fused_computation | custom fusion | bytes 1310784 | tf_op jit(solution)/shard_map/gather | solution.py:355
  66.9 0.3 fusion.7.picked_ref
  67.2 0.0 collective-permute-done.other_ref
  67.2 0.0 copy-start.1
  67.2 1.0 copy-done.1
  68.2 0.0 copy-start.4
  68.2 0.7 copy-done.4
  68.9 9.1 %attend.1 = bf16[16,16,1024]{2,1,0:T(8,128)(2,1)} custom-call(s32[1,128]{1,0:T(1,128)S(1)} %get-tuple-element.82.slot_ref, s32[16,128]{1,0:T(8,128)S(1)} %bitcast.12, bf16[16,16,1280]{2,1,0:T(8,128)(2,1)S(1)} %fusion.7.picked_ref, bf16[1024,256]{1,0:T(8,128)(2,1)S(1)} %bitcast.11, bf16[1024,256]{1,0:T(8,128)(2,1)S(1)} %collective-permute-done.other_ref), custom_call_target="tpu_custom_call" | custom-call | tf_op jit(solution)/shard_map/attend/pallas_call | solution.py:185
  78.0 4.2 %all-to-all-start.3 = ((bf16[16,16,1024]{2,1,0:T(8,128)(2,1)}), bf16[16,16,1024]{2,1,0:T(8,128)(2,1)}, u32[]{:S(2)}, u32[]{:S(2)}) async-start(bf16[16,16,1024]{2,1,0:T(8,128)(2,1)} %attend.1), calls=%async_computation.3 | async-start | bytes 1048576 | tf_op jit(solution)/shard_map/all_to_all | solution.py:358
  82.2 2.1 collective-permute-start.3
  84.3 4.8 %collective-permute-start.2 = (bf16[1024,512]{1,0:T(8,128)(2,1)}, bf16[1024,512]{1,0:T(8,128)(2,1)S(1)}, u32[]{:S(2)}, u32[]{:S(2)}) collective-permute-start(bf16[1024,512]{1,0:T(8,128)(2,1)} %param.14), channel_id=1, source_target_pairs={{2,0},{3,1},{0,2},{1,3},{6,4},{7,5},{4,6},{5,7},{10,8},{11,9},{8,1... | collective-permute-start | bytes 3145736 | tf_op jit(solution)/shard_map/ppermute | solution.py:27
  89.1 3.5 %collective-permute-start.1 = (bf16[1024,512]{1,0:T(8,128)(2,1)}, bf16[1024,512]{1,0:T(8,128)(2,1)}, u32[]{:S(2)}, u32[]{:S(2)}) collective-permute-start(bf16[1024,512]{1,0:T(8,128)(2,1)} %param.14), channel_id=1, source_target_pairs={{1,0},{2,1},{3,2},{0,3},{5,4},{6,5},{7,6},{4,7},{9,8},{10,9},{11,1... | collective-permute-start | bytes 3145736 | tf_op jit(solution)/shard_map/ppermute | solution.py:27
  92.7 17.4 %collective-permute-done.3 = bf16[1024,512]{1,0:T(8,128)(2,1)S(1)} collective-permute-done((bf16[1024,512]{1,0:T(8,128)(2,1)}, bf16[1024,512]{1,0:T(8,128)(2,1)S(1)}, u32[]{:S(2)}, u32[]{:S(2)}) %collective-permute-start.3) | collective-permute-done | bytes 1048608 | tf_op jit(solution)/shard_map/ppermute | solution.py:27
  110.1 22.9 %collective-permute-done.2 = bf16[1024,512]{1,0:T(8,128)(2,1)S(1)} collective-permute-done((bf16[1024,512]{1,0:T(8,128)(2,1)}, bf16[1024,512]{1,0:T(8,128)(2,1)S(1)}, u32[]{:S(2)}, u32[]{:S(2)}) %collective-permute-start.2) | collective-permute-done | bytes 1048608 | tf_op jit(solution)/shard_map/ppermute | solution.py:27
  133.0 1.9 collective-permute-done.1
  134.9 0.0 all-to-all-done.3
  134.9 75.4 %conditional.1 = (bf16[512,512]{1,0:T(8,128)(2,1)S(1)}) conditional(s32[]{:T(128)} %bitcast.1, (s32[1,128]{1,0:T(1,128)S(1)}, bf16[16,16,1024]{2,1,0:T(8,128)(2,1)}, s32[3,128]{1,0:T(4,128)S(1)}, bf16[1024,512]{1,0:T(8,128)(2,1)}, bf16[1024,512]{1,0:T(8,128)(2,1)}, /*index=5*/bf16[1024,512]{1,0:T(8,128)(2,1)S(1)}, ...), branch_computations={%region_0.0_spmd, %region_1.0_spmd, %region_2.0_spmd} | conditional | flops 58982400 | bytes 64487488 | solution.py:360
  134.9 0.0 copy-start.6
  134.9 1.6 settle.3
  136.6 9.4 %all_to_all.22.quarters_ref = bf16[4,24,1024]{2,1,0:T(8,128)(2,1)S(1)} all-to-all(bf16[4,24,1024]{2,1,0:T(8,128)(2,1)S(1)} %settle.3), channel_id=1, replica_groups={{0,1,2,3},{4,5,6,7},{8,9,10,11},{12,13,14,15},{16,17,18,19},{20,21,22,2..., dimensions={0} | all-to-all | bytes 393216 | tf_op jit(solution)/shard_map/cond/branch_0_fun/all_to_all | solution.py:338
  145.9 0.3 join.3
  146.2 55.2 %all-gather.4 = f16[768,4096]{1,0:T(8,128)(2,1)S(1)} all-gather(f16[24,4096]{1,0:T(8,128)(2,1)S(1)} %convert_element_type.24), channel_id=1, replica_groups=mesh['dp'=32,'tensor'=16] {'dp'}, dimensions={0}, use_global_device_ids=true | all-gather | bytes 6488064 | tf_op jit(solution)/shard_map/cond/branch_0_fun/all_gather | solution.py:340
  201.4 2.9 %fusion.1.every_ref = bf16[768,4096]{1,0:T(8,128)(2,1)S(1)} fusion(f16[768,4096]{1,0:T(8,128)(2,1)S(1)} %all-gather.4), kind=kLoop, calls=%fused_computation.6 | loop fusion | flops 22020096 | bytes 12582912 | tf_op jit(solution)/shard_map/cond/branch_0_fun/convert_element_type | solution.py:37
  204.3 0.0 copy-done.6
  204.3 5.5 %project.3 = bf16[512,512]{1,0:T(8,128)(2,1)S(1)} custom-call(s32[3,128]{1,0:T(4,128)S(1)} %get-tuple-element.50.spot_ref, bf16[768,4096]{1,0:T(8,128)(2,1)S(1)} %fusion.1.every_ref, bf16[1024,512]{1,0:T(8,128)(2,1)S(1)} %copy-done.6, bf16[1024,512]{1,0:T(8,128)(2,1)} %get-tuple-element.55.refs_1_, bf16[1024,512]{1,0:T(8,128)(2,1)S(1)} %get-tuple-element.56.refs_2_, ...), custom_call_target="tpu_custom_call" | custom-call | tf_op jit(solution)/shard_map/cond/branch_0_fun/project/pallas_call | solution.py:296
  210.3 14.7 %all_to_all.25.shares_ref = bf16[16,32,512]{2,1,0:T(8,128)(2,1)S(1)} all-to-all(bf16[16,32,512]{2,1,0:T(8,128)(2,1)S(1)} %bitcast.15), channel_id=1, replica_groups=mesh['dp'=32,'tensor'=16] {'tensor'}, dimensions={0} | all-to-all | bytes 1048576 | tf_op jit(solution)/shard_map/all_to_all | solution.py:369
  225.0 0.7 finish.1
  (4 shorter events, 0.1 us)
Async XLA Ops:
  0.0 67.2 %collective-permute-start = (bf16[1024,256]{1,0:T(8,128)(2,1)}, bf16[1024,256]{1,0:T(8,128)(2,1)S(1)}, u32[]{:S(2)}, u32[]{:S(2)}) collective-permute-start(bf16[1024,256]{1,0:T(8,128)(2,1)} %bitcast.10), channel_id=1, source_target_pairs={{0,1},{1,0},{2,3},{3,2},{4,5},{5,4},{6,7},{7,6},{8,9},{9,8},{10,11... | collective-permute-start | bytes 1572872 | tf_op jit(solution)/shard_map/ppermute | solution.py:21
  4.0 1.0 copy-start.2
  5.0 0.9 copy-start.3
  5.9 0.7 copy-start.5
  67.2 1.0 copy-start.1
  68.2 0.7 copy-start.4
  78.0 56.9 %all-to-all-start.3 = ((bf16[16,16,1024]{2,1,0:T(8,128)(2,1)}), bf16[16,16,1024]{2,1,0:T(8,128)(2,1)}, u32[]{:S(2)}, u32[]{:S(2)}) async-start(bf16[16,16,1024]{2,1,0:T(8,128)(2,1)} %attend.1), calls=%async_computation.3 | async-start | bytes 1048576 | tf_op jit(solution)/shard_map/all_to_all | solution.py:358
  82.2 27.9 %collective-permute-start.3 = (bf16[1024,512]{1,0:T(8,128)(2,1)}, bf16[1024,512]{1,0:T(8,128)(2,1)S(1)}, u32[]{:S(2)}, u32[]{:S(2)}) collective-permute-start(bf16[1024,512]{1,0:T(8,128)(2,1)} %param.14), channel_id=1, source_target_pairs={{3,0},{0,1},{1,2},{2,3},{7,4},{4,5},{5,6},{6,7},{11,8},{8,9},{9,10... | collective-permute-start | bytes 3145736 | tf_op jit(solution)/shard_map/ppermute | solution.py:27
  84.3 48.7 %collective-permute-start.2 = (bf16[1024,512]{1,0:T(8,128)(2,1)}, bf16[1024,512]{1,0:T(8,128)(2,1)S(1)}, u32[]{:S(2)}, u32[]{:S(2)}) collective-permute-start(bf16[1024,512]{1,0:T(8,128)(2,1)} %param.14), channel_id=1, source_target_pairs={{2,0},{3,1},{0,2},{1,3},{6,4},{7,5},{4,6},{5,7},{10,8},{11,9},{8,1... | collective-permute-start | bytes 3145736 | tf_op jit(solution)/shard_map/ppermute | solution.py:27
  89.1 45.8 %collective-permute-start.1 = (bf16[1024,512]{1,0:T(8,128)(2,1)}, bf16[1024,512]{1,0:T(8,128)(2,1)}, u32[]{:S(2)}, u32[]{:S(2)}) collective-permute-start(bf16[1024,512]{1,0:T(8,128)(2,1)} %param.14), channel_id=1, source_target_pairs={{1,0},{2,1},{3,2},{0,3},{5,4},{6,5},{7,6},{4,7},{9,8},{10,9},{11,1... | collective-permute-start | bytes 3145736 | tf_op jit(solution)/shard_map/ppermute | solution.py:27
  134.9 69.4 %copy-start.6 = (bf16[1024,512]{1,0:T(8,128)(2,1)S(1)}, bf16[1024,512]{1,0:T(8,128)(2,1)}, u32[]{:S(2)}) copy-start(bf16[1024,512]{1,0:T(8,128)(2,1)} %get-tuple-element.54.refs_0_) | copy-start | bytes 3145732 | tf_op jit(solution)/shard_map/cond

commit v8 on v6

--- a/solution.py
+++ b/solution.py
@@ -12,6 +12,7 @@
 PAIR = 16
 BLOCK = 8
 ROWS = (6, 7, 8, 16)
+HALF = 8
 NEG = -1e30
 LIFT = 2.0**59
 
@@ -196,64 +197,113 @@
     )(slot, parents, picked, own, other)
 
 
-def settle_kernel(source_ref, spread_ref, out_ref):
-    for k in range(out_ref.shape[0]):
-        out_ref[k] = encode(spread_ref[source_ref[0, k]].astype(jnp.float32))
+def settle_kernel(source_ref, spread_ref, kept_ref, sent_ref):
+    odd = (lax.axis_index("tensor") & 1) == 1
+    for k in range(kept_ref.shape[0]):
+        rows = spread_ref[source_ref[0, k]].astype(jnp.float32)
+        lower, upper = rows[:HALF], rows[HALF:]
+        kept_ref[k] = jnp.where(odd, upper, lower).astype(jnp.bfloat16)
+        sent_ref[k] = jnp.where(odd, lower, upper).astype(jnp.bfloat16)
 
 
 def settle(source, spread, count):
     vmem = pl.BlockSpec(memory_space=pltpu.VMEM)
+    part = jax.ShapeDtypeStruct((count, HALF, spread.shape[2]), jnp.bfloat16)
     return pl.pallas_call(
         settle_kernel,
-        out_shape=jax.ShapeDtypeStruct((count, *spread.shape[1:]), jnp.float32),
+        out_shape=(part, part),
         grid_spec=pltpu.PrefetchScalarGridSpec(
-            num_scalar_prefetch=1, grid=(), in_specs=[vmem], out_specs=vmem
+            num_scalar_prefetch=1, grid=(), in_specs=[vmem], out_specs=(vmem, vmem)
         ),
         compiler_params=pltpu.CompilerParams(vmem_limit_bytes=12 * 1024 * 1024),
         name="settle",
     )(source, spread)
 
 
-def project_kernel(choice, spot_ref, every_ref, weight_ref, out_ref):
-    lanes = out_ref.shape[0]
-    share = spot_ref.shape[1] // lanes
-    for lane in range(lanes):
+def join_kernel(kept_ref, got_ref, out_ref):
+    depth = kept_ref.shape[2]
+    out_ref[:, :, :depth] = encode(kept_ref[...].astype(jnp.float32))
+    out_ref[:, :, depth:] = encode(got_ref[...].astype(jnp.float32))
+
+
+def join(kept, got):
+    vmem = pl.BlockSpec(memory_space=pltpu.VMEM)
+    count, rows, depth = kept.shape
+    return pl.pallas_call(
+        join_kernel,
+        out_shape=jax.ShapeDtypeStruct((count, rows, 2 * depth), jnp.float32),
+        in_specs=[vmem] * 2,
+        out_specs=vmem,
+        compiler_params=pltpu.CompilerParams(vmem_limit_bytes=12 * 1024 * 1024),
+        name="join",
+    )(kept, got)
+
+
+def project_kernel(choice, spot_ref, every_ref, own_ref, other_ref, out_ref):
+    depth = own_ref.shape[0]
+    requests = spot_ref.shape[1]
+    step = 32
+    for start in range(0, requests, step):
         block = jnp.concatenate(
-            [every_ref[spot_ref[choice, lane * share + r]] for r in range(share)], axis=0
+            [every_ref[spot_ref[choice, start + r]] for r in range(step)], axis=0
         )
-        out_ref[lane] = jnp.dot(
-            block, weight_ref[...], preferred_element_type=jnp.float32
-        ).astype(jnp.bfloat16)
-
-
-def project(choice, spot, every, weight, lanes):
-    requests, nodes = spot.shape[1], every.shape[1]
-    columns = weight.shape[1]
+        product = jnp.dot(block[:, :depth], own_ref[...], preferred_element_type=jnp.float32)
+        product += jnp.dot(block[:, depth:], other_ref[...], preferred_element_type=jnp.float32)
+        out_ref[start * HALF : (start + step) * HALF] = product.astype(jnp.bfloat16)
+
+
+def project(choice, spot, every, own, other):
+    requests = spot.shape[1]
+    columns = own.shape[1]
     vmem = pl.BlockSpec(memory_space=pltpu.VMEM)
     return pl.pallas_call(
         functools.partial(project_kernel, choice),
-        out_shape=jax.ShapeDtypeStruct((lanes, requests // lanes * nodes, columns), jnp.bfloat16),
+        out_shape=jax.ShapeDtypeStruct((requests * HALF, columns), jnp.bfloat16),
         grid_spec=pltpu.PrefetchScalarGridSpec(
-            num_scalar_prefetch=1, grid=(), in_specs=[vmem] * 2, out_specs=vmem
+            num_scalar_prefetch=1, grid=(), in_specs=[vmem] * 3, out_specs=vmem
         ),
-        compiler_params=pltpu.CompilerParams(vmem_limit_bytes=16 * 1024 * 1024),
+        compiler_params=pltpu.CompilerParams(vmem_limit_bytes=24 * 1024 * 1024),
         name="project",
-    )(spot, every, weight)
-
-
-def share_rows(choice, lanes, source, spread, spot, weight):
-    settled = settle(source, spread, ROWS[choice])
-    every = lax.all_gather(settled.astype(jnp.float16), "dp", axis=0, tiled=True)
-    return project(choice, spot, decode(every), weight, lanes)
+    )(spot, every, own, other)
+
+
+def finish_kernel(shares_ref, out_ref):
+    lanes = shares_ref.shape[0]
+    for half in range(2):
+        total = shares_ref[half].astype(jnp.float32)
+        for lane in range(half + 2, lanes, 2):
+            total += shares_ref[lane].astype(jnp.float32)
+        out_ref[:, half * HALF : (half + 1) * HALF] = total.astype(jnp.bfloat16)
+
+
+def finish(shares):
+    lanes, rows, half, columns = shares.shape
+    vmem = pl.BlockSpec(memory_space=pltpu.VMEM)
+    return pl.pallas_call(
+        finish_kernel,
+        out_shape=jax.ShapeDtypeStruct((rows, 2 * half, columns), jnp.bfloat16),
+        in_specs=[vmem],
+        out_specs=vmem,
+        compiler_params=pltpu.CompilerParams(vmem_limit_bytes=12 * 1024 * 1024),
+        name="finish",
+    )(shares)
+
+
+def share_rows(choice, source, spread, spot, own, other):
+    kept, sent = settle(source, spread, ROWS[choice])
+    joined = join(kept, swapped(sent, "tensor", 0))
+    every = lax.all_gather(joined.astype(jnp.float16), "dp", axis=0, tiled=True)
+    return project(choice, spot, decode(every), own, other)
 
 
 def local(queries, tree_kv, prefix_kv, request_holder, parents, out_weight):
     lanes = lax.axis_size("tensor")
     groups = lax.axis_size("dp")
     requests = request_holder.shape[0]
-    nodes = queries.shape[1]
     own_half = prefix_kv[0, 0]
-    other_half = swapped(own_half, "tensor", 0)
+    other_half, other_weight = lax.optimization_barrier(
+        (swapped(own_half, "tensor", 0), swapped(out_weight, "tensor", 0))
+    )
     packed, slot, index, spot, source, most = pack(queries, tree_kv, request_holder)
     packed = lax.all_gather(packed.astype(jnp.float16), "dp", axis=0, tiled=True)
     picked = decode(packed.at[index[0, :CAP]].get(mode="promise_in_bounds"))
@@ -262,15 +312,15 @@
     spread = lax.all_to_all(attended, "dp", 0, 0, axis_index_groups=blocks, tiled=True)
     partial = lax.switch(
         most[0, 0],
-        [functools.partial(share_rows, choice, lanes) for choice in range(len(ROWS))],
+        [functools.partial(share_rows, choice) for choice in range(len(ROWS))],
         source,
         spread,
         spot,
         out_weight,
-    )
-    shares = lax.all_to_all(partial, "tensor", 0, 0, tiled=True)
-    total = jnp.sum(shares.astype(jnp.float32), axis=0).astype(jnp.bfloat16)
-    return total.reshape(requests // lanes, nodes, out_weight.shape[1])
+        other_weight,
+    )
+    partial = partial.reshape(lanes, requests // lanes, HALF, out_weight.shape[1])
+    return finish(lax.all_to_all(partial, "tensor", 0, 0, tiled=True))
 
 
 def solution(mesh):

time: 201 us -> 186 us (0.925)
  blocking collectives: 147 us -> 130 us
  other arithmetic: 9.47 us -> 3.26 us
  starting transfers between devices: 7.56 us -> 12.7 us
  waiting for transfers between devices: 14.5 us -> 16.6 us
    all_to_all x1, blocking collectives: 33.4 us -> 22.3 us  [local(): return finish(lax.all_to_all(partial, 'tensor', 0, 0, tiled=True))]
    all_gather x1, blocking collectives: 57.9 us -> 52.3 us  [share_rows(): every = lax.all_gather(joined.astype(jnp.float16), 'dp', axis=0, tiled=True)]
    ppermute x1 -> x3, starting transfers between devices: 4.02 us -> 9.15 us  [swapped(): lax.ppermute(x, axis, [(i, i ^ 1 << bit) for i in range(lax.axis_size(axi...]
    convert_element_type x2, other arithmetic: 6.84 us -> 3.2 us  [decode(): return (x * jnp.abs(x) * (x * (1.0 / LIFT) * x)).astype(jnp.bfloat16)]
    reduce_sum x1 -> x0, other arithmetic: 2.57 us -> none  [local(): total = jnp.sum(shares.astype(jnp.float32), axis=0).astype(jnp.bfloat16)]
    ppermute x1 -> x3, waiting for transfers between devices: 0.01 us -> 2.15 us  [swapped(): lax.ppermute(x, axis, [(i, i ^ 1 << bit) for i in range(lax.axis_size(axi...]
  transfers between devices with their start and end apart: 2 -> 4, of which waited for: 1 -> 2; matrix products, arithmetic and copies ran while one was open for 2% -> 2% of each run, Pallas kernels for 0% -> 1%
where the time goes in v8:
time: 186 us
  blocking collectives  130 us (70%)
  waiting for transfers between devices  16.6 us (9%)
  Pallas kernels  14.5 us (8%)
  starting transfers between devices  12.7 us (7%)
  local copies, waits for them, and re-layouts  7.56 us (4%)
  other arithmetic  3.26 us (2%)
    all_gather x1, blocking collectives, local(): lax.all_gather(packed.astype(jnp.float16), 'dp', axis=0, tiled=True)  55.8 us
    all_gather x1, blocking collectives, share_rows(): every = lax.all_gather(joined.astype(jnp.float16), 'dp', axis=0, tiled=True)  52.3 us
    all_to_all x1, blocking collectives, local(): return finish(lax.all_to_all(partial, 'tensor', 0, 0, tiled=True))  22.3 us
    all_to_all x1, waiting for transfers between devices, local(): lax.all_to_all(attended, 'dp', 0, 0, axis_index_groups=blocks, tiled=True)  14.5 us
    ppermute x3, starting transfers between devices, swapped(): lax.ppermute(x, axis, [(i, i ^ 1 << bit) for i in range(lax.axis_size(axi...  9.15 us
    pallas_call x1, Pallas kernels, attend(): pl.pallas_call(attend_kernel, out_shape=jax.ShapeDtypeStruct((CAP, nodes,...  9.05 us
    unnamed x10, local copies, waits for them, and re-layouts  4.23 us
  transfers between devices with their start and end apart: 4, of which 2 were waited for; matrix products, arithmetic and copies ran while one was open for 2% of the time, Pallas kernels for 1%

profile of v8, /device:TPU:1, one launch (start us, length us, event | category | flops | bytes accessed | tf_op | source)
XLA Modules:
  0.0 185.8 jit_solution(17311708194892070354)
XLA Ops:
  0.0 4.0 %collective-permute-start.4 = (bf16[1024,256]{1,0:T(8,128)(2,1)}, bf16[1024,256]{1,0:T(8,128)(2,1)S(1)}, u32[]{:S(2)}, u32[]{:S(2)}) collective-permute-start(bf16[1024,256]{1,0:T(8,128)(2,1)} %bitcast.10), channel_id=1, source_target_pairs={{0,1},{1,0},{2,3},{3,2},{4,5},{5,4},{6,7},{7,6},{8,9},{9,8},{10,11... | collective-permute-start | bytes 1572872 | tf_op jit(solution)/shard_map/ppermute | solution.py:21
  4.0 1.9 %collective-permute-start.5 = (bf16[1024,512]{1,0:T(8,128)(2,1)}, bf16[1024,512]{1,0:T(8,128)(2,1)S(1)}, u32[]{:S(2)}, u32[]{:S(2)}) collective-permute-start(bf16[1024,512]{1,0:T(8,128)(2,1)} %param.15), channel_id=1, source_target_pairs={{0,1},{1,0},{2,3},{3,2},{4,5},{5,4},{6,7},{7,6},{8,9},{9,8},{10,11... | collective-permute-start | bytes 3145736 | tf_op jit(solution)/shard_map/ppermute | solution.py:21
  6.0 0.0 copy-start.2
  6.0 0.9 copy-done.2
  6.9 0.0 copy-start.3
  6.9 0.9 copy-done.3
  7.8 0.0 copy-start.5
  7.8 0.7 copy-done.5
  8.5 1.0 pack.1
  9.5 55.8 %all-gather.9 = f16[128,16,1280]{2,1,0:T(8,128)(2,1)} all-gather(f16[4,16,1280]{2,1,0:T(8,128)(2,1)S(1)} %convert_element_type.45), channel_id=1, replica_groups=mesh['dp'=32,'tensor'=16] {'dp'}, dimensions={0}, use_global_device_ids=true | all-gather | bytes 5406720 | tf_op jit(solution)/shard_map/all_gather | solution.py:308
  65.3 3.3 %gather_fusion = f16[16,16,1280]{2,1,0:T(8,128)(2,1)S(1)} fusion(f16[128,16,1280]{2,1,0:T(8,128)(2,1)} %all-gather.9, s32[1024]{0:T(1024)S(1)} %pad_clamp_fusion), kind=kCustom, calls=%fused_computation | custom fusion | bytes 1310784 | tf_op jit(solution)/shard_map/gather | solution.py:309
  68.6 0.3 fusion.9.picked_ref
  68.9 0.0 collective-permute-done.4.other_ref
  68.9 0.0 collective-permute-done.5
  69.0 0.0 copy-start.1
  69.0 1.0 copy-done.1
  70.0 0.0 copy-start.4
  70.0 0.7 copy-done.4
  70.7 9.0 %attend.1 = bf16[16,16,1024]{2,1,0:T(8,128)(2,1)} custom-call(s32[1,128]{1,0:T(1,128)S(1)} %get-tuple-element.88.slot_ref, s32[16,128]{1,0:T(8,128)S(1)} %bitcast.12, bf16[16,16,1280]{2,1,0:T(8,128)(2,1)S(1)} %fusion.9.picked_ref, bf16[1024,256]{1,0:T(8,128)(2,1)S(1)} %bitcast.11, bf16[1024,256]{1,0:T(8,128)(2,1)S(1)} %collective-permute-done.4.other_ref), custom_call_target="tpu_custom_call" | custom-call | tf_op jit(solution)/shard_map/attend/pallas_call | solution.py:179
  79.7 3.5 %all-to-all-start = ((bf16[16,16,1024]{2,1,0:T(8,128)(2,1)}), bf16[16,16,1024]{2,1,0:T(8,128)(2,1)S(1)}, u32[]{:S(2)}, u32[]{:S(2)}) async-start(bf16[16,16,1024]{2,1,0:T(8,128)(2,1)} %attend.1), calls=%async_computation | async-start | bytes 1048576 | tf_op jit(solution)/shard_map/all_to_all | solution.py:312
  83.3 14.5 %all-to-all-done = bf16[16,16,1024]{2,1,0:T(8,128)(2,1)S(1)} async-done(((bf16[16,16,1024]{2,1,0:T(8,128)(2,1)}), bf16[16,16,1024]{2,1,0:T(8,128)(2,1)S(1)}, u32[]{:S(2)}, u32[]{:S(2)}) %all-to-all-start) | async-done | bytes 524320 | tf_op jit(solution)/shard_map/all_to_all | solution.py:312
  97.8 64.9 %conditional.1 = (bf16[1024,512]{1,0:T(8,128)(2,1)S(1)}) conditional(s32[]{:T(128)} %bitcast.1, (s32[1,128]{1,0:T(1,128)S(1)}, bf16[16,16,1024]{2,1,0:T(8,128)(2,1)S(1)}, s32[4,128]{1,0:T(4,128)S(1)}, bf16[1024,512]{1,0:T(8,128)(2,1)}, bf16[1024,512]{1,0:T(8,128)(2,1)S(1)}) %tuple.19, (s32[1,128]{1,0:T(1,128)S(1)}, ...), branch_computations={%region_0.0_spmd, %region_1.0_spmd, %region_2.0_spmd, %region_3.0_... | conditional | flops 58982400 | bytes 64487528 | solution.py:313
  97.8 0.0 copy-start.6
  97.8 0.6 settle.4
  98.4 3.2 %collective-permute-start = (bf16[6,8,1024]{2,1,0:T(8,128)(2,1)S(1)}, bf16[6,8,1024]{2,1,0:T(8,128)(2,1)S(1)}, u32[]{:S(2)}, u32[]{:S(2)}) collective-permute-start(bf16[6,8,1024]{2,1,0:T(8,128)(2,1)S(1)} %get-tuple-element.54), channel_id=1, source_target_pairs={{0,1},{1,0},{2,3},{3,2},{4,5},{5,4},{6,7},{7,6},{8,9},{9,8},{10,11... | collective-permute-start | bytes 294920 | tf_op jit(solution)/shard_map/cond/branch_0_fun/ppermute | solution.py:21
  101.6 2.1 %collective-permute-done.got_ref = bf16[6,8,1024]{2,1,0:T(8,128)(2,1)S(1)} collective-permute-done((bf16[6,8,1024]{2,1,0:T(8,128)(2,1)S(1)}, bf16[6,8,1024]{2,1,0:T(8,128)(2,1)S(1)}, u32[]{:S(2)}, u32[]{:S(2)}) %collective-permute-start) | collective-permute-done | bytes 98336 | tf_op jit(solution)/shard_map/cond/branch_0_fun/ppermute | solution.py:21
  103.7 0.3 join.4
  104.0 52.3 %all-gather.5 = f16[192,8,2048]{2,1,0:T(8,128)(2,1)S(1)} all-gather(f16[6,8,2048]{2,1,0:T(8,128)(2,1)S(1)} %convert_element_type.30), channel_id=1, replica_groups=mesh['dp'=32,'tensor'=16] {'dp'}, dimensions={0}, use_global_device_ids=true | all-gather | bytes 6488064 | tf_op jit(solution)/shard_map/cond/branch_0_fun/all_gather | solution.py:295
  156.3 2.9 %fusion.1.every_ref = bf16[192,8,2048]{2,1,0:T(8,128)(2,1)S(1)} fusion(f16[192,8,2048]{2,1,0:T(8,128)(2,1)S(1)} %all-gather.5), kind=kLoop, calls=%fused_computation.6 | loop fusion | flops 22020096 | bytes 12582912 | tf_op jit(solution)/shard_map/cond/branch_0_fun/convert_element_type | solution.py:31
  159.3 0.0 copy-done.6
  159.3 2.9 %project.4 = bf16[1024,512]{1,0:T(8,128)(2,1)S(1)} custom-call(s32[4,128]{1,0:T(4,128)S(1)} %get-tuple-element.48.spot_ref, bf16[192,8,2048]{2,1,0:T(8,128)(2,1)S(1)} %fusion.1.every_ref, bf16[1024,512]{1,0:T(8,128)(2,1)S(1)} %copy-done.6, bf16[1024,512]{1,0:T(8,128)(2,1)S(1)} %get-tuple-element.56.other_ref), custom_call_target="tpu_custom_call" | custom-call | tf_op jit(solution)/shard_map/cond/branch_0_fun/project/pallas_call | solution.py:259
  162.7 22.3 %all_to_all.10.shares_ref = bf16[16,8,8,512]{3,2,1,0:T(8,128)(2,1)S(1)} all-to-all(bf16[16,8,8,512]{3,2,1,0:T(8,128)(2,1)S(1)} %bitcast.15), channel_id=1, replica_groups=mesh['dp'=32,'tensor'=16] {'tensor'}, dimensions={0} | all-to-all | bytes 2097152 | tf_op jit(solution)/shard_map/all_to_all | solution.py:323
  185.0 0.8 finish.1
  (4 shorter events, 0.1 us)
Async XLA Ops:
  0.0 68.9 %collective-permute-start.4 = (bf16[1024,256]{1,0:T(8,128)(2,1)}, bf16[1024,256]{1,0:T(8,128)(2,1)S(1)}, u32[]{:S(2)}, u32[]{:S(2)}) collective-permute-start(bf16[1024,256]{1,0:T(8,128)(2,1)} %bitcast.10), channel_id=1, source_target_pairs={{0,1},{1,0},{2,3},{3,2},{4,5},{5,4},{6,7},{7,6},{8,9},{9,8},{10,11... | collective-permute-start | bytes 1572872 | tf_op jit(solution)/shard_map/ppermute | solution.py:21
  4.0 64.9 %collective-permute-start.5 = (bf16[1024,512]{1,0:T(8,128)(2,1)}, bf16[1024,512]{1,0:T(8,128)(2,1)S(1)}, u32[]{:S(2)}, u32[]{:S(2)}) collective-permute-start(bf16[1024,512]{1,0:T(8,128)(2,1)} %param.15), channel_id=1, source_target_pairs={{0,1},{1,0},{2,3},{3,2},{4,5},{5,4},{6,7},{7,6},{8,9},{9,8},{10,11... | collective-permute-start | bytes 3145736 | tf_op jit(solution)/shard_map/ppermute | solution.py:21
  6.0 1.0 copy-start.2
  6.9 0.9 copy-start.3
  7.8 0.7 copy-start.5
  69.0 1.0 copy-start.1
  70.0 0.7 copy-start.4
  79.7 18.0 %all-to-all-start = ((bf16[16,16,1024]{2,1,0:T(8,128)(2,1)}), bf16[16,16,1024]{2,1,0:T(8,128)(2,1)S(1)}, u32[]{:S(2)}, u32[]{:S(2)}) async-start(bf16[16,16,1024]{2,1,0:T(8,128)(2,1)} %attend.1), calls=%async_computation | async-start | bytes 1048576 | tf_op jit(solution)/shard_map/all_to_all | solution.py:312
  97.8 61.5 %copy-start.6 = (bf16[1024,512]{1,0:T(8,128)(2,1)S(1)}, bf16[1024,512]{1,0:T(8,128)(2,1)}, u32[]{:S(2)}) copy-start(bf16[1024,512]{1,0:T(8,128)(2,1)} %get-tuple-element.55.own_ref) | copy-start | bytes 3145732 | tf_op jit(solution)/shard_map/cond
  98.4 5.4 %collective-permute-start = (bf16[6,8,1024]{2,1,0:T(8,128)(2,1)S(1)}, bf16[6,8,1024]{2,1,0:T(8,128)(2,1)S(1)}, u32[]{:S(2)}, u32[]{:S(2)}) collective-permute-start(bf16[6,8,1024]{2,1,0:T(8,128)(2,1)S(1)} %get-tuple-element.54), channel_id=1, source_target_pairs={{0,1},{1,0},{2,3},{3,2},{4,5},{5,4},{6,7},{7,6},{8,9},{9,8},{10,11... | collective-permute-start | bytes 294920 | tf_op jit(solution)/shard_map/cond/branch_0_fun/ppermute | solution.py:21
